TPU v7x, 128 devices: a whole 4x4x4 slice. The times are simulated.
128 devices in a mesh: rows: 64 (over x, y_lo, z, core), frames: 2 (over y_hi).
Axes of the slice: x: 4, y: 4 (y_hi: 2, y_lo: 2; y = y_hi * 2 + y_lo), z: 4, core: 2. Of those that a mesh axis runs over, the one named last changes fastest.
Arguments:
- latents: bfloat16 [4, 128, 48, 640], P('frames', 'rows'), may hold values from -6 to 6
- previous: bfloat16 [4, 128, 48, 640], P('frames', 'rows'), may hold values from -6 to 6
- stale_normed: bfloat16 [4, 128, 48, 640], P('frames', 'rows'), may hold values from -6 to 6
- norm_gains: float32 [3, 640], replicated, may hold values from 0.1 to 1.9
- logit_scale: float32 [2, 10], replicated, may hold values from 1 to 10
- conv_weight: bfloat16 [9, 640, 640], replicated, may hold values from -0.078125 to 0.078125
- attn_weight: bfloat16 [640, 1920], replicated, may hold values from -0.25 to 0.25
- attn_out: bfloat16 [640, 640], replicated, may hold values from -0.25 to 0.25
- temporal_weight: bfloat16 [640, 1920], replicated, may hold values from -0.25 to 0.25
- temporal_out: bfloat16 [640, 640], replicated, may hold values from -0.25 to 0.25
- ff_in: bfloat16 [640, 5120], replicated, may hold values from -0.25 to 0.25
- ff_out: bfloat16 [2560, 640], replicated, may hold values from -0.125 to 0.125
Outputs:
- block_out: float32 [4, 128, 48, 640], P('frames', 'rows')
All inputs are finite; a program needn't handle non-finite values.
Results may differ from a plain program's by a relative error of at most 0.019.
The roundings to bfloat16 on the way count: a program that leaves them out, or rounds other values in their place, can miss the bound.
Values may be sent and summed in bfloat16 or wider, within the bound.
A program may use at most 256 MiB of HBM per device.

v0:
```python
import math

import jax
import jax.numpy as jnp
from jax import lax
from jax.sharding import PartitionSpec as P

HEADS = 10
HEAD_DIM = 64


NEG = -1e30
EPS = 1e-05


def extended(cells, sides, width):
    for axis, dim in sides:
        count = lax.axis_size(axis)
        ends = count - 1
        head = lax.slice_in_dim(cells, 0, width, axis=dim)
        tail = lax.slice_in_dim(cells, cells.shape[dim] - width, cells.shape[dim], axis=dim)
        cells = jnp.concatenate(
            [
                lax.ppermute(tail, axis, [(i, (i + 1) % count) for i in range(ends)]),
                cells,
                lax.ppermute(head, axis, [((i + 1) % count, i) for i in range(ends)]),
            ],
            axis=dim,
        )
    return cells


def layer_norm(values, gain):
    centre = values - jnp.mean(values, axis=-1, keepdims=True)
    spread = jnp.mean(centre * centre, axis=-1, keepdims=True)
    return (centre * lax.rsqrt(spread + EPS) * gain).astype(jnp.bfloat16)


def heads_of(tensor):
    return tensor.reshape(tensor.shape[0], -1, HEADS, HEAD_DIM)


def attend_block(carry, queries, keys, values, keep, scale):
    peak, total, accum = carry
    scores = (
        jnp.einsum("fqhd,fkhd->fhqk", queries, keys, preferred_element_type=jnp.float32)
        * scale[None, :, None, None]
    )
    if keep is not None:
        scores = jnp.where(keep, scores, NEG)
    new_peak = jnp.maximum(peak, jnp.max(scores, axis=-1))
    weights = jnp.exp(scores - new_peak[..., None])
    if keep is not None:
        weights = jnp.where(keep, weights, 0.0)
    factor = jnp.exp(peak - new_peak)
    total = total * factor + jnp.sum(weights, axis=-1)
    accum = accum * factor[..., None] + jnp.einsum(
        "fhqk,fkhd->fhqd", weights.astype(jnp.bfloat16), values, preferred_element_type=jnp.float32
    )
    return (new_peak, total, accum)


def block_size(piece_rows, cols_here):
    target = max(1, 1024 // cols_here)
    best = 1
    for option in range(1, min(target, piece_rows) + 1):
        if piece_rows % option == 0:
            best = option
    return best


def scan_rows(state, pieces, make, queries, scale, own_start, own_rows):
    frames_here, piece_rows, cols_here, width = pieces[0].shape
    step = block_size(piece_rows, cols_here)
    count = piece_rows // step
    stacked = tuple(
        (
            jnp.moveaxis(item.reshape(frames_here, count, step, cols_here, width), 1, 0)
            for item in pieces
        )
    )

    def visit(carry, inputs):
        index = inputs[0]
        blocks = tuple((item.reshape(frames_here, step * cols_here, width) for item in inputs[1:]))
        keys_blk, values_blk = make(blocks)
        row_ids = index * step + jnp.arange(step, dtype=jnp.int32)
        keep_rows = (row_ids < own_start) | (row_ids >= own_start + own_rows)
        keep = jnp.broadcast_to(keep_rows[:, None], (step, cols_here)).reshape(-1)
        return (
            attend_block(carry, queries, heads_of(keys_blk), heads_of(values_blk), keep, scale),
            None,
        )

    state, unused = lax.scan(visit, state, (jnp.arange(count, dtype=jnp.int32),) + stacked)
    return state


def temporal_mix(queries, keys, values, scale):
    shape = queries.shape
    query_heads = queries.reshape(shape[0], -1, HEADS, HEAD_DIM)
    key_heads = keys.reshape(keys.shape[0], -1, HEADS, HEAD_DIM)
    value_heads = values.reshape(keys.shape[0], -1, HEADS, HEAD_DIM)
    scores = (
        jnp.einsum("anhd,bnhd->nhab", query_heads, key_heads, preferred_element_type=jnp.float32)
        * scale[None, :, None, None]
    )
    peak = jnp.max(scores, axis=-1, keepdims=True)
    weights = jnp.exp(scores - peak)
    total = jnp.sum(weights, axis=-1)
    mixed = jnp.einsum(
        "nhab,bnhd->anhd",
        weights.astype(jnp.bfloat16),
        value_heads,
        preferred_element_type=jnp.float32,
    )
    mixed = mixed / jnp.transpose(total, (2, 0, 1))[..., None]
    return mixed.astype(jnp.bfloat16).reshape(shape)


def body(
    latents,
    previous,
    stale_normed,
    norm_gains,
    logit_scale,
    conv_weight,
    attn_weight,
    attn_out,
    temporal_weight,
    temporal_out,
    ff_in,
    ff_out,
):
    frames_here, rows_here, cols_here, width = latents.shape
    padded = extended(previous, (("rows", 1),), 1)
    field = jnp.concatenate([padded[:, :1], latents, padded[:, rows_here + 1 :]], axis=1)
    field = jax.nn.silu(field.astype(jnp.float32)).astype(jnp.bfloat16)
    field = jnp.pad(field, ((0, 0), (0, 0), (1, 1), (0, 0)))
    conv_sum = jnp.zeros(latents.shape, jnp.float32)
    for row_step in range(3):
        for col_step in range(3):
            window = field[:, row_step : row_step + rows_here, col_step : col_step + cols_here]
            conv_sum = conv_sum + jnp.dot(
                window, conv_weight[row_step * 3 + col_step], preferred_element_type=jnp.float32
            )
    first = latents.astype(jnp.float32) + conv_sum
    normed = layer_norm(first, norm_gains[0])
    triple = jnp.dot(normed, attn_weight, preferred_element_type=jnp.float32).astype(jnp.bfloat16)
    queries = heads_of(triple[..., :width])
    keys_now = heads_of(triple[..., width : 2 * width])
    values_now = heads_of(triple[..., 2 * width :])
    scale = logit_scale[0] / math.sqrt(HEAD_DIM)
    count_q = rows_here * cols_here
    carry = (
        jnp.full((frames_here, HEADS, count_q), NEG, jnp.float32),
        jnp.zeros((frames_here, HEADS, count_q), jnp.float32),
        jnp.zeros((frames_here, HEADS, count_q, HEAD_DIM), jnp.float32),
    )
    carry = attend_block(carry, queries, keys_now, values_now, None, scale)
    own_start = lax.axis_index("rows") * rows_here
    kv_weight = attn_weight[:, width:]
    both = jnp.dot(stale_normed, kv_weight, preferred_element_type=jnp.float32).astype(jnp.bfloat16)
    stale_keys = both[..., :width]
    stale_values = both[..., width:]

    def make_keys(blocks):
        return (blocks[0], blocks[1])

    carry = scan_rows(
        carry,
        (
            lax.all_gather(stale_keys, "rows", axis=1, tiled=True),
            lax.all_gather(stale_values, "rows", axis=1, tiled=True),
        ),
        make_keys,
        queries,
        scale,
        own_start,
        rows_here,
    )
    peak, total, accum = carry
    spatial_mix = accum / total[..., None]
    spatial_mix = (
        jnp.transpose(spatial_mix, (0, 2, 1, 3)).reshape(latents.shape).astype(jnp.bfloat16)
    )
    second = first + jnp.dot(spatial_mix, attn_out, preferred_element_type=jnp.float32)
    normed_two = layer_norm(second, norm_gains[1])
    time_scale = logit_scale[1] / math.sqrt(HEAD_DIM)
    groups = lax.axis_size("frames")
    split_view = normed_two.reshape(frames_here, rows_here, groups, cols_here // groups, width)
    projected = jnp.dot(
        lax.all_to_all(split_view, "frames", split_axis=2, concat_axis=0, tiled=True),
        temporal_weight,
        preferred_element_type=jnp.float32,
    ).astype(jnp.bfloat16)
    spread_out = temporal_mix(
        projected[..., :width],
        projected[..., width : 2 * width],
        projected[..., 2 * width :],
        time_scale,
    )
    returned = lax.all_to_all(spread_out, "frames", split_axis=0, concat_axis=2, tiled=True)
    mixed_time = returned.reshape(latents.shape)
    third = second + jnp.dot(mixed_time, temporal_out, preferred_element_type=jnp.float32)
    normed_three = layer_norm(third, norm_gains[2])
    both = jnp.dot(normed_three, ff_in, preferred_element_type=jnp.float32)
    half = ff_out.shape[0]
    ff_hidden = (both[..., :half] * jax.nn.gelu(both[..., half:], approximate=False)).astype(
        jnp.bfloat16
    )
    return third + jnp.dot(ff_hidden, ff_out, preferred_element_type=jnp.float32)


def solution(mesh):
    return jax.shard_map(
        body,
        mesh=mesh,
        in_specs=(
            P("frames", "rows", None, None),
            P("frames", "rows", None, None),
            P("frames", "rows", None, None),
            P(),
            P(),
            P(),
            P(),
            P(),
            P(),
            P(),
            P(),
            P(),
        ),
        out_specs=P("frames", "rows", None, None),
        check_vma=False,
    )
```

profile of v0, /device:TPU:0, one launch (start us, length us, event | category | flops | bytes accessed | tf_op | source)
XLA Modules:
  0.0 676.7 jit_solution(7750896063570852545)
XLA Ops:
  13.8 4.3 collective-permute-done.1
  46.0 88.5 %all-gather.3.cloned.1.call-done = bf16[2,128,48,640]{3,2,1,0:T(8,128)(2,1)} async-done(((bf16[2,2,48,640]{3,2,1,0:T(8,128)(2,1)}), bf16[2,128,48,640]{3,2,1,0:T(8,128)(2,1)}) %all-gather.3.cloned.1.call-update) | async-done | bytes 15728656 | tf_op jit(solution)/shard_map/all_gather | solution.py:173
  134.5 43.8 %copy.44 = bf16[2,8,16,48,640]{3,2,4,0,1:T(8,128)(2,1)} copy(bf16[2,8,16,48,640]{4,3,2,1,0:T(8,128)(2,1)} %bitcast.208) | data formatting | bytes 31457280 | tf_op jit(solution)/shard_map/reshape | solution.py:78
  178.3 79.0 %all-gather.5.cloned.1.call-done = bf16[2,128,48,640]{3,2,1,0:T(8,128)(2,1)} async-done(((bf16[2,2,48,640]{3,2,1,0:T(8,128)(2,1)}), bf16[2,128,48,640]{3,2,1,0:T(8,128)(2,1)}) %all-gather.5.cloned.1.call-update) | async-done | bytes 15728656 | tf_op jit(solution)/shard_map/all_gather | solution.py:174
  257.3 43.7 %copy.45 = bf16[2,8,16,48,640]{3,2,4,0,1:T(8,128)(2,1)} copy(bf16[2,8,16,48,640]{4,3,2,1,0:T(8,128)(2,1)} %bitcast.209) | data formatting | bytes 31457280 | tf_op jit(solution)/shard_map/reshape | solution.py:78
  301.1 314.7 %while.15 = (s32[]{:T(128)}, f32[2,10,96]{2,1,0:T(8,128)S(1)}, f32[2,10,96]{2,1,0:T(8,128)S(1)}, f32[2,10,96,64]{2,3,1,0:T(8,128)}, s32[8]{0:T(128)S(1)}, /*inde...) while((s32[]{:T(128)}, f32[2,10,96]{2,1,0:T(8,128)S(1)}, ...), condition=%wide.region_7.8_spmd, body=%wide.region_4.7_spmd.sunk | while | flops 396906304 | bytes 62305112 | solution.py:95
  302.6 9.8 %constant_dynamic-slice_fusion.3 = (bf16[1,2,16,48,640]{3,2,4,1,0:T(8,128)(2,1)}, bf16[1,2,16,48,640]{3,2,4,1,0:T(8,128)(2,1)}) fusion(bf16[8,2,16,48,640]{3,2,4,1,0:T(8,128)(2,1)} %get-tuple-element.286, s32[]{:T(128)} %get-tuple-element.263, bf16[8,2,16,48,640]{3,2,4,1,0:T(8,128)(2,1)} %get-tuple-element.283), kind=kLoop, calls=%fused_computation.14.clone.1 | loop fusion | bytes 7864324 | tf_op jit(solution)/shard_map/while/body/jit(dynamic_index_in_dim)/dynamic_slice | solution.py:95
  312.4 8.4 %reshape.166 = bf16[2,768,10,64]{1,3,2,0:T(8,128)(2,1)} reshape(bf16[1,2,16,48,640]{3,2,4,1,0:T(8,128)(2,1)} %get-tuple-element.244) | data formatting | bytes 3932160 | tf_op jit(solution)/shard_map/while/body/eval_jaxpr/reshape;while/body/eval_jaxpr/reshape | solution.py:40
  320.8 2.6 bitcast_reduce_fusion.2
  326.0 8.5 %reshape.167 = bf16[2,768,10,64]{1,3,2,0:T(8,128)(2,1)} reshape(bf16[1,2,16,48,640]{3,2,4,1,0:T(8,128)(2,1)} %get-tuple-element.248) | data formatting | bytes 3932160 | tf_op jit(solution)/shard_map/while/body/eval_jaxpr/reshape;while/body/eval_jaxpr/reshape | solution.py:40
  334.5 5.9 fusion.194
  341.9 9.8 %constant_dynamic-slice_fusion.3 = (bf16[1,2,16,48,640]{3,2,4,1,0:T(8,128)(2,1)}, bf16[1,2,16,48,640]{3,2,4,1,0:T(8,128)(2,1)}) fusion(bf16[8,2,16,48,640]{3,2,4,1,0:T(8,128)(2,1)} %get-tuple-element.286, s32[]{:T(128)} %get-tuple-element.263, bf16[8,2,16,48,640]{3,2,4,1,0:T(8,128)(2,1)} %get-tuple-element.283), kind=kLoop, calls=%fused_computation.14.clone.1 | loop fusion | bytes 7864324 | tf_op jit(solution)/shard_map/while/body/jit(dynamic_index_in_dim)/dynamic_slice | solution.py:95
  351.7 8.4 %reshape.166 = bf16[2,768,10,64]{1,3,2,0:T(8,128)(2,1)} reshape(bf16[1,2,16,48,640]{3,2,4,1,0:T(8,128)(2,1)} %get-tuple-element.244) | data formatting | bytes 3932160 | tf_op jit(solution)/shard_map/while/body/eval_jaxpr/reshape;while/body/eval_jaxpr/reshape | solution.py:40
  360.1 2.6 bitcast_reduce_fusion.2
  365.3 8.5 %reshape.167 = bf16[2,768,10,64]{1,3,2,0:T(8,128)(2,1)} reshape(bf16[1,2,16,48,640]{3,2,4,1,0:T(8,128)(2,1)} %get-tuple-element.248) | data formatting | bytes 3932160 | tf_op jit(solution)/shard_map/while/body/eval_jaxpr/reshape;while/body/eval_jaxpr/reshape | solution.py:40
  373.8 5.9 fusion.194
  381.3 9.8 %constant_dynamic-slice_fusion.3 = (bf16[1,2,16,48,640]{3,2,4,1,0:T(8,128)(2,1)}, bf16[1,2,16,48,640]{3,2,4,1,0:T(8,128)(2,1)}) fusion(bf16[8,2,16,48,640]{3,2,4,1,0:T(8,128)(2,1)} %get-tuple-element.286, s32[]{:T(128)} %get-tuple-element.263, bf16[8,2,16,48,640]{3,2,4,1,0:T(8,128)(2,1)} %get-tuple-element.283), kind=kLoop, calls=%fused_computation.14.clone.1 | loop fusion | bytes 7864324 | tf_op jit(solution)/shard_map/while/body/jit(dynamic_index_in_dim)/dynamic_slice | solution.py:95
  391.0 8.4 %reshape.166 = bf16[2,768,10,64]{1,3,2,0:T(8,128)(2,1)} reshape(bf16[1,2,16,48,640]{3,2,4,1,0:T(8,128)(2,1)} %get-tuple-element.244) | data formatting | bytes 3932160 | tf_op jit(solution)/shard_map/while/body/eval_jaxpr/reshape;while/body/eval_jaxpr/reshape | solution.py:40
  399.5 2.6 bitcast_reduce_fusion.2
  404.7 8.5 %reshape.167 = bf16[2,768,10,64]{1,3,2,0:T(8,128)(2,1)} reshape(bf16[1,2,16,48,640]{3,2,4,1,0:T(8,128)(2,1)} %get-tuple-element.248) | data formatting | bytes 3932160 | tf_op jit(solution)/shard_map/while/body/eval_jaxpr/reshape;while/body/eval_jaxpr/reshape | solution.py:40
  413.1 5.9 fusion.194
  420.6 9.8 %constant_dynamic-slice_fusion.3 = (bf16[1,2,16,48,640]{3,2,4,1,0:T(8,128)(2,1)}, bf16[1,2,16,48,640]{3,2,4,1,0:T(8,128)(2,1)}) fusion(bf16[8,2,16,48,640]{3,2,4,1,0:T(8,128)(2,1)} %get-tuple-element.286, s32[]{:T(128)} %get-tuple-element.263, bf16[8,2,16,48,640]{3,2,4,1,0:T(8,128)(2,1)} %get-tuple-element.283), kind=kLoop, calls=%fused_computation.14.clone.1 | loop fusion | bytes 7864324 | tf_op jit(solution)/shard_map/while/body/jit(dynamic_index_in_dim)/dynamic_slice | solution.py:95
  430.4 8.4 %reshape.166 = bf16[2,768,10,64]{1,3,2,0:T(8,128)(2,1)} reshape(bf16[1,2,16,48,640]{3,2,4,1,0:T(8,128)(2,1)} %get-tuple-element.244) | data formatting | bytes 3932160 | tf_op jit(solution)/shard_map/while/body/eval_jaxpr/reshape;while/body/eval_jaxpr/reshape | solution.py:40
  438.8 2.6 bitcast_reduce_fusion.2
  444.0 8.5 %reshape.167 = bf16[2,768,10,64]{1,3,2,0:T(8,128)(2,1)} reshape(bf16[1,2,16,48,640]{3,2,4,1,0:T(8,128)(2,1)} %get-tuple-element.248) | data formatting | bytes 3932160 | tf_op jit(solution)/shard_map/while/body/eval_jaxpr/reshape;while/body/eval_jaxpr/reshape | solution.py:40
  452.5 5.9 fusion.194
  459.9 9.8 %constant_dynamic-slice_fusion.3 = (bf16[1,2,16,48,640]{3,2,4,1,0:T(8,128)(2,1)}, bf16[1,2,16,48,640]{3,2,4,1,0:T(8,128)(2,1)}) fusion(bf16[8,2,16,48,640]{3,2,4,1,0:T(8,128)(2,1)} %get-tuple-element.286, s32[]{:T(128)} %get-tuple-element.263, bf16[8,2,16,48,640]{3,2,4,1,0:T(8,128)(2,1)} %get-tuple-element.283), kind=kLoop, calls=%fused_computation.14.clone.1 | loop fusion | bytes 7864324 | tf_op jit(solution)/shard_map/while/body/jit(dynamic_index_in_dim)/dynamic_slice | solution.py:95
  469.7 8.4 %reshape.166 = bf16[2,768,10,64]{1,3,2,0:T(8,128)(2,1)} reshape(bf16[1,2,16,48,640]{3,2,4,1,0:T(8,128)(2,1)} %get-tuple-element.244) | data formatting | bytes 3932160 | tf_op jit(solution)/shard_map/while/body/eval_jaxpr/reshape;while/body/eval_jaxpr/reshape | solution.py:40
  478.2 2.6 bitcast_reduce_fusion.2
  483.4 8.5 %reshape.167 = bf16[2,768,10,64]{1,3,2,0:T(8,128)(2,1)} reshape(bf16[1,2,16,48,640]{3,2,4,1,0:T(8,128)(2,1)} %get-tuple-element.248) | data formatting | bytes 3932160 | tf_op jit(solution)/shard_map/while/body/eval_jaxpr/reshape;while/body/eval_jaxpr/reshape | solution.py:40
  491.8 5.9 fusion.194
  499.3 9.8 %constant_dynamic-slice_fusion.3 = (bf16[1,2,16,48,640]{3,2,4,1,0:T(8,128)(2,1)}, bf16[1,2,16,48,640]{3,2,4,1,0:T(8,128)(2,1)}) fusion(bf16[8,2,16,48,640]{3,2,4,1,0:T(8,128)(2,1)} %get-tuple-element.286, s32[]{:T(128)} %get-tuple-element.263, bf16[8,2,16,48,640]{3,2,4,1,0:T(8,128)(2,1)} %get-tuple-element.283), kind=kLoop, calls=%fused_computation.14.clone.1 | loop fusion | bytes 7864324 | tf_op jit(solution)/shard_map/while/body/jit(dynamic_index_in_dim)/dynamic_slice | solution.py:95
  509.0 8.4 %reshape.166 = bf16[2,768,10,64]{1,3,2,0:T(8,128)(2,1)} reshape(bf16[1,2,16,48,640]{3,2,4,1,0:T(8,128)(2,1)} %get-tuple-element.244) | data formatting | bytes 3932160 | tf_op jit(solution)/shard_map/while/body/eval_jaxpr/reshape;while/body/eval_jaxpr/reshape | solution.py:40
  517.5 2.6 bitcast_reduce_fusion.2
  522.7 8.5 %reshape.167 = bf16[2,768,10,64]{1,3,2,0:T(8,128)(2,1)} reshape(bf16[1,2,16,48,640]{3,2,4,1,0:T(8,128)(2,1)} %get-tuple-element.248) | data formatting | bytes 3932160 | tf_op jit(solution)/shard_map/while/body/eval_jaxpr/reshape;while/body/eval_jaxpr/reshape | solution.py:40
  531.1 5.9 fusion.194
  538.6 9.8 %constant_dynamic-slice_fusion.3 = (bf16[1,2,16,48,640]{3,2,4,1,0:T(8,128)(2,1)}, bf16[1,2,16,48,640]{3,2,4,1,0:T(8,128)(2,1)}) fusion(bf16[8,2,16,48,640]{3,2,4,1,0:T(8,128)(2,1)} %get-tuple-element.286, s32[]{:T(128)} %get-tuple-element.263, bf16[8,2,16,48,640]{3,2,4,1,0:T(8,128)(2,1)} %get-tuple-element.283), kind=kLoop, calls=%fused_computation.14.clone.1 | loop fusion | bytes 7864324 | tf_op jit(solution)/shard_map/while/body/jit(dynamic_index_in_dim)/dynamic_slice | solution.py:95
  548.4 8.4 %reshape.166 = bf16[2,768,10,64]{1,3,2,0:T(8,128)(2,1)} reshape(bf16[1,2,16,48,640]{3,2,4,1,0:T(8,128)(2,1)} %get-tuple-element.244) | data formatting | bytes 3932160 | tf_op jit(solution)/shard_map/while/body/eval_jaxpr/reshape;while/body/eval_jaxpr/reshape | solution.py:40
  562.0 8.5 %reshape.167 = bf16[2,768,10,64]{1,3,2,0:T(8,128)(2,1)} reshape(bf16[1,2,16,48,640]{3,2,4,1,0:T(8,128)(2,1)} %get-tuple-element.248) | data formatting | bytes 3932160 | tf_op jit(solution)/shard_map/while/body/eval_jaxpr/reshape;while/body/eval_jaxpr/reshape | solution.py:40
  570.5 5.9 fusion.194
  577.9 9.8 %constant_dynamic-slice_fusion.3 = (bf16[1,2,16,48,640]{3,2,4,1,0:T(8,128)(2,1)}, bf16[1,2,16,48,640]{3,2,4,1,0:T(8,128)(2,1)}) fusion(bf16[8,2,16,48,640]{3,2,4,1,0:T(8,128)(2,1)} %get-tuple-element.286, s32[]{:T(128)} %get-tuple-element.263, bf16[8,2,16,48,640]{3,2,4,1,0:T(8,128)(2,1)} %get-tuple-element.283), kind=kLoop, calls=%fused_computation.14.clone.1 | loop fusion | bytes 7864324 | tf_op jit(solution)/shard_map/while/body/jit(dynamic_index_in_dim)/dynamic_slice | solution.py:95
  587.7 8.4 %reshape.166 = bf16[2,768,10,64]{1,3,2,0:T(8,128)(2,1)} reshape(bf16[1,2,16,48,640]{3,2,4,1,0:T(8,128)(2,1)} %get-tuple-element.244) | data formatting | bytes 3932160 | tf_op jit(solution)/shard_map/while/body/eval_jaxpr/reshape;while/body/eval_jaxpr/reshape | solution.py:40
  601.4 8.5 %reshape.167 = bf16[2,768,10,64]{1,3,2,0:T(8,128)(2,1)} reshape(bf16[1,2,16,48,640]{3,2,4,1,0:T(8,128)(2,1)} %get-tuple-element.248) | data formatting | bytes 3932160 | tf_op jit(solution)/shard_map/while/body/eval_jaxpr/reshape;while/body/eval_jaxpr/reshape | solution.py:40
  609.8 5.9 fusion.194
  622.9 10.8 %all_to_all.30 = bf16[2,2,2,24,640]{4,3,1,0,2:T(8,128)(2,1)S(1)} all-to-all(bf16[2,2,2,24,640]{4,3,1,0,2:T(8,128)(2,1)S(1)} %copy.47), channel_id=1, replica_groups=mesh['rows'=64,'frames'=2] {'frames'}, dimensions={2} | all-to-all | bytes 491520 | tf_op jit(solution)/shard_map/all_to_all | solution.py:193
  648.5 9.0 %all_to_all.31 = bf16[4,2,1,24,640]{4,3,1,2,0:T(8,128)(2,1)S(1)} all-to-all(bf16[4,2,1,24,640]{4,3,1,2,0:T(8,128)(2,1)S(1)} %bitcast.213), channel_id=1, replica_groups=mesh['rows'=64,'frames'=2] {'frames'}, dimensions={0} | all-to-all | bytes 491520 | tf_op jit(solution)/shard_map/all_to_all | solution.py:203
  659.5 4.6 fusion.13
  664.1 5.7 fusion.43
  (168 shorter events, 91.0 us)
Async XLA Ops:
  6.5 657.6 %copy-start = (bf16[2560,640]{1,0:T(8,128)(2,1)S(1)}, bf16[2560,640]{1,0:T(8,128)(2,1)}, u32[]{:S(2)}) copy-start(bf16[2560,640]{1,0:T(8,128)(2,1)} %param.25) | copy-start | bytes 9830404
  6.5 3.9 copy-start.8
  6.5 7.2 %copy-start.11 = (f32[2,10]{1,0:T(2,128)S(1)}, f32[2,10]{1,0:T(2,128)}, u32[]{:S(2)}) copy-start(f32[2,10]{1,0:T(2,128)} %param.18) | copy-start | bytes 244
  6.5 7.2 %copy-start.10 = (f32[3,640]{1,0:T(4,128)S(1)}, f32[3,640]{1,0:T(4,128)}, u32[]{:S(2)}) copy-start(f32[3,640]{1,0:T(4,128)} %param.17) | copy-start | bytes 23044
  6.5 128.0 %all-gather.3.cloned.1.call-start = ((), (), s32[]{:S(2)}) async-start(), calls=%async_computation.2 | async-start | bytes 15974400 | tf_op jit(solution)/shard_map/all_gather | solution.py:173
  9.7 247.6 %all-gather.5.cloned.1.call-start = ((), (), s32[]{:S(2)}) async-start(), calls=%async_computation.3 | async-start | bytes 15974400 | tf_op jit(solution)/shard_map/all_gather | solution.py:174
  11.2 2.7 collective-permute-start
  12.5 5.7 collective-permute-start.1
  18.1 7.9 %copy-start.4 = (bf16[9,640,640]{2,1,0:T(8,128)(2,1)S(1)}, bf16[9,640,640]{2,1,0:T(8,128)(2,1)}, u32[]{:S(2)}) copy-start(bf16[9,640,640]{2,1,0:T(8,128)(2,1)} %param.19) | copy-start | bytes 22118404
  26.0 1.0 copy-start.9
  27.8 1.9 copy-start.5
  28.3 2.2 copy-start.3
  43.2 1.7 copy-start.6
  323.4 2.6 copy-start.1
  362.8 2.6 copy-start.1
  402.1 2.6 copy-start.1
  441.4 2.6 copy-start.1
  480.8 2.6 copy-start.1
  520.1 2.6 copy-start.1
  559.4 2.6 copy-start.1
  598.8 2.6 copy-start.1
  619.8 13.9 %copy-start.12 = (bf16[640,1920]{1,0:T(8,128)(2,1)S(1)}, bf16[640,1920]{1,0:T(8,128)(2,1)}, u32[]{:S(2)}) copy-start(bf16[640,1920]{1,0:T(8,128)(2,1)} %param.22) | copy-start | bytes 7372804
  621.9 0.8 copy-start.2
  641.2 3.5 copy-start.7
Sparse Core Ops, SparseCore 0:
  9.8 124.6 all-gather.2
  136.2 121.1 all-gather.4
where the time goes:
time: 683 us; the launch traced here: 677 us
  local copies, waits for them, and re-layouts  341 us (50%)
  waiting for transfers between devices  173 us (25%)
  matrix products  102 us (15%)
  blocking collectives  19.8 us (3%)
  other arithmetic  19.2 us (3%)
  between operations  13.8 us (2%)
    reshape x19, local copies, waits for them, and re-layouts, heads_of(): return tensor.reshape(tensor.shape[0], -1, HEADS, HEAD_DIM)  142 us
    all_gather x1, waiting for transfers between devices, body(): lax.all_gather(stale_keys, 'rows', axis=1, tiled=True)  88.5 us
    reshape x2, local copies, waits for them, and re-layouts, scan_rows(): item.reshape(frames_here, count, step, cols_here, width)  87.5 us
    dynamic_slice x16, local copies, waits for them, and re-layouts, scan_rows(): lax.scan(visit, state, (jnp.arange(count, dtype=jnp.int32),) + stacked)  83.5 us
    all_gather x1, waiting for transfers between devices, body(): lax.all_gather(stale_values, 'rows', axis=1, tiled=True)  79 us
    dot_general x9, matrix products, attend_block(): jnp.einsum('fhqk,fkhd->fhqd', weights.astype(jnp.bfloat16), values, prefe...  48.7 us
    dot_general x9, matrix products, attend_block(): jnp.einsum('fqhd,fkhd->fhqk', queries, keys, preferred_element_type=jnp.f...  22.5 us
    reduce_sum x9, other arithmetic, attend_block(): total = total * factor + jnp.sum(weights, axis=-1)  14.1 us
  transfers between devices with their start and end apart: 4, of which 3 were waited for; matrix products, arithmetic and copies ran while one was open for 10% of the time, Pallas kernels for 0%

commit v1 on v0

v1 whole, which is shorter than its diff:
```python
import functools
import math

import jax
import jax.numpy as jnp
from jax import lax
from jax.experimental import pallas as pl
from jax.experimental.pallas import tpu as pltpu
from jax.sharding import PartitionSpec as P

HEADS = 10
HEAD_DIM = 64
NEG = -1e30
EPS = 1e-05
F32 = jnp.float32
BF16 = jnp.bfloat16
MESH = pl.DeviceIdType.MESH
NT = (((1,), (1,)), ((), ()))
PATCH = 96
QUERIES = 384
PAIRS = 3
HALF = 384


def extended(cells, sides, width):
    for axis, dim in sides:
        count = lax.axis_size(axis)
        ends = count - 1
        head = lax.slice_in_dim(cells, 0, width, axis=dim)
        tail = lax.slice_in_dim(cells, cells.shape[dim] - width, cells.shape[dim], axis=dim)
        cells = jnp.concatenate(
            [
                lax.ppermute(tail, axis, [(i, (i + 1) % count) for i in range(ends)]),
                cells,
                lax.ppermute(head, axis, [((i + 1) % count, i) for i in range(ends)]),
            ],
            axis=dim,
        )
    return cells


def layer_norm(values, gain):
    centre = values - jnp.mean(values, axis=-1, keepdims=True)
    spread = jnp.mean(centre * centre, axis=-1, keepdims=True)
    return (centre * lax.rsqrt(spread + EPS) * gain).astype(BF16)


def temporal_mix(queries, keys, values, scale):
    shape = queries.shape
    query_heads = queries.reshape(shape[0], -1, HEADS, HEAD_DIM)
    key_heads = keys.reshape(keys.shape[0], -1, HEADS, HEAD_DIM)
    value_heads = values.reshape(keys.shape[0], -1, HEADS, HEAD_DIM)
    scores = (
        jnp.einsum("anhd,bnhd->nhab", query_heads, key_heads, preferred_element_type=F32)
        * scale[None, :, None, None]
    )
    peak = jnp.max(scores, axis=-1, keepdims=True)
    weights = jnp.exp(scores - peak)
    total = jnp.sum(weights, axis=-1)
    mixed = jnp.einsum(
        "nhab,bnhd->anhd", weights.astype(BF16), value_heads, preferred_element_type=F32
    )
    mixed = mixed / jnp.transpose(total, (2, 0, 1))[..., None]
    return mixed.astype(BF16).reshape(shape)


def spatial_kernel(
    stale_ref, q_ref, kv_ref, w_ref, out_ref,
    xall, q_in, kv_in, q_heads, kv, acc, peak, total, result,
    recv, sent, sent_loop, q_recv, q_sent, kv_recv, kv_sent, r_recv, r_sent, local,
):
    row = lax.axis_index("rows")
    part = lax.axis_index("frames")
    core = row % 2
    z = (row // 2) % 4
    y = (row // 8) % 2
    x = row // 16

    def device(x, y, z, core):
        return (((x * 2 + y) * 4 + z) * 2 + core, part)

    def ring(along_first, step):
        dx = step * (1 - core) if along_first else step * core
        dz = step * core if along_first else step * (1 - core)
        return device((x + dx + 4) % 4, y, (z + dz + 4) % 4, core)

    a_up, a_down = ring(True, 1), ring(True, -1)
    b_up, b_down = ring(False, 1), ring(False, -1)
    mate = device(x, y, z, 1 - core)
    across = device(x, 1 - y, z, core)
    quad = [(0, 1, across), (1, 0, mate), (1, 1, device(x, 1 - y, z, 1 - core))]

    barrier = pltpu.get_barrier_semaphore()
    for other in (a_up, a_down, b_up, b_down, across, mate, quad[2][2]):
        pl.semaphore_signal(barrier, inc=1, device_id=other, device_id_type=MESH)
    pl.semaphore_wait(barrier, 7)

    started = []

    def push(src, dst, send_sem, recv_sem, to):
        copy = pltpu.make_async_remote_copy(
            src_ref=src, dst_ref=dst, send_sem=send_sem, recv_sem=recv_sem,
            device_id=to, device_id_type=MESH,
        )
        copy.start()
        return copy

    def send(src, slot, to):
        da, dc, db, dy = slot
        dst = xall.at[da, dc, db] if dy is None else xall.at[da, dc, db, dy]
        started.append(push(src, dst, sent.at[len(started)], recv.at[da, dc, db, dy or 0], to))

    def arrived(da, dc, db, dy=None):
        dst = xall.at[da, dc, db] if dy is None else xall.at[da, dc, db, dy]
        pltpu.make_async_remote_copy(
            src_ref=dst, dst_ref=dst, send_sem=recv.at[da, dc, db, dy or 0],
            recv_sem=recv.at[da, dc, db, dy or 0], device_id=mate, device_id_type=MESH,
        ).wait_recv()

    own = stale_ref.at[y]
    send(stale_ref.at[1 - y], (0, 0, 0, 1), across)
    for slot, to in (
        ((0, 1, 0, 0), mate), ((3, 0, 0, 0), a_up), ((1, 0, 0, 0), a_down),
        ((0, 0, 3, 0), b_up), ((0, 0, 1, 0), b_down),
    ):
        send(own, slot, to)
    keep_own = pltpu.make_async_copy(own, xall.at[0, 0, 0, 0], local.at[0])
    keep_own.start()
    q_copies = []
    for dc, dy, to in quad:
        q_copies.append(push(
            q_ref.at[(y + dy) % 2, (core + dc) % 2], q_in.at[dc * 2 + dy],
            q_sent.at[dc * 2 + dy], q_recv.at[dc * 2 + dy], to,
        ))
    kv_copies = []
    for dc, dy, to in quad:
        kv_copies.append(push(
            kv_ref.at[(y + dy) % 2, (core + dc) % 2], kv_in.at[dc * 2 + dy],
            kv_sent.at[dc * 2 + dy], kv_recv.at[dc * 2 + dy], to,
        ))
    keep_q = pltpu.make_async_copy(q_ref.at[y, core], q_in.at[0], local.at[1])
    keep_q.start()
    keep_kv = pltpu.make_async_copy(kv_ref.at[y, core], kv_in.at[0], local.at[2])
    keep_kv.start()

    arrived(0, 0, 0, 1)
    second = xall.at[0, 0, 0, 1]
    for slot, to in (
        ((0, 1, 0, 1), mate), ((3, 0, 0, 1), a_up), ((1, 0, 0, 1), a_down),
        ((0, 0, 3, 1), b_up), ((0, 0, 1, 1), b_down),
    ):
        send(second, slot, to)

    keep_q.wait()
    for copy in q_copies:
        copy.wait_recv()
    lane = lax.broadcasted_iota(jnp.int32, (QUERIES, 128), 1)
    for pair in range(PAIRS):
        both = q_in[:, :, 128 * pair : 128 * pair + 128].reshape(QUERIES, 128)
        zero = jnp.zeros_like(both)
        q_heads[2 * pair] = jnp.where(lane < HEAD_DIM, both, zero)
        if pair < 2:
            q_heads[2 * pair + 1] = jnp.where(lane < HEAD_DIM, zero, both)
    acc[...] = jnp.zeros_like(acc)
    total[...] = jnp.zeros_like(total)
    peak[...] = jnp.full_like(peak, NEG)
    weight = w_ref.at[core]

    def project(rows, first):
        kv[first : first + rows.shape[0]] = jnp.dot(
            rows, weight[...], preferred_element_type=F32
        ).astype(BF16)

    def attend(keys, masked, hooks):
        for pair in range(PAIRS):
            k = kv[:keys, 128 * pair : 128 * pair + 128]
            v = kv[:keys, HALF + 128 * pair : HALF + 128 * pair + 128]
            factors, parts = [], []
            for head in range(2 * pair, min(2 * pair + 2, 5)):
                s = lax.dot_general(q_heads[head], k, NT, preferred_element_type=F32)
                if masked:
                    q_patch = lax.broadcasted_iota(jnp.int32, (QUERIES, keys), 0) // PATCH
                    k_patch = lax.broadcasted_iota(jnp.int32, (QUERIES, keys), 1) // PATCH
                    drop = ((k_patch < 4) & (k_patch == q_patch)) | (
                        (k_patch >= 4) & (k_patch != q_patch + 4)
                    )
                    s = jnp.where(drop, NEG, s)
                old = peak[head]
                new = jnp.maximum(old, jnp.max(s, axis=1, keepdims=True))
                factor = jnp.exp2(old - new)
                w = jnp.exp2(s - new[:, :1])
                total[head] = total[head] * factor + jnp.sum(w, axis=1, keepdims=True)
                peak[head] = new
                factors.append(factor)
                parts.append(jnp.dot(w.astype(BF16), v, preferred_element_type=F32))
                if head in hooks:
                    hooks[head]()
            if len(parts) == 2:
                acc[pair] = acc[pair] * jnp.where(lane < HEAD_DIM, *factors) + jnp.where(
                    lane < HEAD_DIM, *parts
                )
            else:
                acc[pair] = acc[pair] * factors[0] + parts[0]

    def loop_copies(da):
        plan = (
            (xall.at[da, 0, 3, 0], xall.at[da, 0, 2, 0], recv.at[da, 0, 2, 0], b_up),
            (xall.at[da, 0, 1, 1], xall.at[da, 0, 2, 1], recv.at[da, 0, 2, 1], b_down),
            (xall.at[da, 0, 3], xall.at[da, 1, 3], recv.at[da, 1, 3, 0], mate),
            (xall.at[da, 0, 1], xall.at[da, 1, 1], recv.at[da, 1, 1, 0], mate),
            (xall.at[da, 0, 2], xall.at[da, 1, 2], recv.at[da, 1, 2, 0], mate),
        )
        return [
            pltpu.make_async_remote_copy(
                src_ref=src, dst_ref=dst, send_sem=sent_loop.at[da, i], recv_sem=sem,
                device_id=to, device_id_type=MESH,
            )
            for i, (src, dst, sem, to) in enumerate(plan)
        ]

    def along_b_first(da, split):
        copies = loop_copies(da)
        for db in (3, 1):
            if split:
                arrived(da, 0, db, 0)
                arrived(da, 0, db, 1)
            else:
                arrived(da, 0, db)
        for copy in copies[:4]:
            copy.start()

    def along_b_second(da):
        arrived(da, 0, 2, 0)
        arrived(da, 0, 2, 1)
        loop_copies(da)[4].start()

    def along_a_first():
        for da in (3, 1):
            arrived(da, 0, 0, 0)
            arrived(da, 0, 0, 1)
        send(xall.at[3, 0, 0, 0], (2, 0, 0, 0), a_up)
        send(xall.at[1, 0, 0, 1], (2, 0, 0, 1), a_down)
        for da in (1, 3):
            spread(da)

    def spread(da):
        chunk = xall.at[da, 0, 0]
        send(chunk, (da, 0, 3, None), b_up)
        send(chunk, (da, 0, 1, None), b_down)
        send(chunk, (da, 1, 0, None), mate)

    def along_a_second():
        arrived(2, 0, 0, 0)
        arrived(2, 0, 0, 1)
        spread(2)

    keep_own.wait()
    arrived(0, 1, 0, 0)
    arrived(0, 1, 0, 1)
    for dc in range(2):
        project(xall[0, dc, 0].reshape(2 * PATCH, -1), dc * 2 * PATCH)
    keep_kv.wait()
    for copy in kv_copies:
        copy.wait_recv()
    kv[4 * PATCH : 8 * PATCH] = kv_in[...].reshape(4 * PATCH, -1)
    along_a_first()
    attend(
        8 * PATCH, True,
        {1: lambda: along_b_first(0, True), 2: along_a_second, 3: lambda: along_b_second(0)},
    )

    for db in (3, 1, 2):
        arrived(0, 1, db)
    for dc in range(2):
        project(xall[0, dc, 1:4].reshape(6 * PATCH, -1), dc * 6 * PATCH)
    attend(
        12 * PATCH, False,
        {0: lambda: along_b_first(1, False), 3: lambda: along_b_second(1)},
    )

    def line(da, carry):
        for db in (0, 3, 1, 2):
            arrived(da, 1, db)
        for dc in range(2):
            project(xall[da, dc].reshape(8 * PATCH, -1), dc * 8 * PATCH)

        def more_first():
            @pl.when(da < 3)
            def _():
                along_b_first(da + 1, False)

        def more_second():
            @pl.when(da < 3)
            def _():
                along_b_second(da + 1)

        attend(16 * PATCH, False, {0: more_first, 3: more_second})
        return carry

    lax.fori_loop(1, 4, line, 0)

    for pair in range(PAIRS):
        below = total[2 * pair]
        if pair < 2:
            below = jnp.where(lane < HEAD_DIM, below, total[2 * pair + 1])
        mixed = (acc[pair] / below).astype(BF16)
        result[:, :, 128 * pair : 128 * pair + 128] = mixed.reshape(4, PATCH, 128)
    r_copies = []
    for dc, dy, to in quad:
        r_copies.append(push(
            result.at[dc * 2 + dy], out_ref.at[y, core],
            r_sent.at[dc * 2 + dy], r_recv.at[dc * 2 + dy], to,
        ))
    keep = pltpu.make_async_copy(result.at[0], out_ref.at[y, core], local.at[3])
    keep.start()
    keep.wait()
    for copy in r_copies:
        copy.wait_recv()
    for copy in started + q_copies + kv_copies + r_copies:
        copy.wait_send()
    for da in range(4):
        for copy in loop_copies(da):
            copy.wait_send()


def spatial(stale, q, kv, weight):
    vmem = pl.BlockSpec(memory_space=pltpu.VMEM)
    dma = pltpu.SemaphoreType.DMA
    return pl.pallas_call(
        spatial_kernel,
        out_shape=jax.ShapeDtypeStruct((2, 2, PATCH, HALF), BF16),
        in_specs=[vmem] * 4,
        out_specs=vmem,
        scratch_shapes=[
            pltpu.VMEM((4, 2, 4, 2, PATCH, 640), BF16),
            pltpu.VMEM((4, PATCH, HALF), BF16),
            pltpu.VMEM((4, PATCH, 2 * HALF), BF16),
            pltpu.VMEM((5, QUERIES, 128), BF16),
            pltpu.VMEM((16 * PATCH, 2 * HALF), BF16),
            pltpu.VMEM((PAIRS, QUERIES, 128), F32),
            pltpu.VMEM((5, QUERIES, 128), F32),
            pltpu.VMEM((5, QUERIES, 128), F32),
            pltpu.VMEM((4, PATCH, HALF), BF16),
            dma((4, 2, 4, 2)),
            dma((22,)),
            dma((4, 5)),
            dma((4,)),
            dma((4,)),
            dma((4,)),
            dma((4,)),
            dma((4,)),
            dma((4,)),
            dma((4,)),
        ],
        compiler_params=pltpu.CompilerParams(
            collective_id=0, has_side_effects=True, vmem_limit_bytes=48 << 20
        ),
        name="spatial",
    )(stale, q, kv, weight)


def half_columns(weight):
    count = weight.shape[1] // 640
    split = weight.reshape(640, count, 2, 320)
    split = jnp.pad(split, ((0, 0), (0, 0), (0, 0), (0, 64)))
    return jnp.transpose(split, (2, 0, 1, 3)).reshape(2, 640, count * HALF)


def body(
    latents,
    previous,
    stale_normed,
    norm_gains,
    logit_scale,
    conv_weight,
    attn_weight,
    attn_out,
    temporal_weight,
    temporal_out,
    ff_in,
    ff_out,
):
    frames_here, rows_here, cols_here, width = latents.shape
    padded = extended(previous, (("rows", 1),), 1)
    field = jnp.concatenate([padded[:, :1], latents, padded[:, rows_here + 1 :]], axis=1)
    field = jax.nn.silu(field.astype(F32)).astype(BF16)
    field = jnp.pad(field, ((0, 0), (0, 0), (1, 1), (0, 0)))
    conv_sum = jnp.zeros(latents.shape, F32)
    for row_step in range(3):
        for col_step in range(3):
            window = field[:, row_step : row_step + rows_here, col_step : col_step + cols_here]
            conv_sum = conv_sum + jnp.dot(
                window, conv_weight[row_step * 3 + col_step], preferred_element_type=F32
            )
    first = latents.astype(F32) + conv_sum
    normed = layer_norm(first, norm_gains[0]).reshape(2, PATCH, width)
    halves = half_columns(attn_weight)
    triple = jnp.einsum("fpc,hcd->fhpd", normed, halves, preferred_element_type=F32)
    scale = logit_scale[0] * (math.log2(math.e) / math.sqrt(HEAD_DIM))
    lanes = jnp.pad(jnp.repeat(scale, HEAD_DIM).reshape(2, 320), ((0, 0), (0, 64)))
    q = (triple[..., :HALF] * lanes[None, :, None, :]).astype(BF16)
    kv_now = triple[..., HALF:].astype(BF16)
    mixed = spatial(
        stale_normed.reshape(2, PATCH, width), q, kv_now, halves[:, :, HALF:]
    )
    spatial_mix = jnp.concatenate([mixed[:, 0, :, :320], mixed[:, 1, :, :320]], axis=-1)
    spatial_mix = spatial_mix.reshape(latents.shape)
    second = first + jnp.dot(spatial_mix, attn_out, preferred_element_type=F32)
    normed_two = layer_norm(second, norm_gains[1])
    time_scale = logit_scale[1] / math.sqrt(HEAD_DIM)
    groups = lax.axis_size("frames")
    split_view = normed_two.reshape(frames_here, rows_here, groups, cols_here // groups, width)
    projected = jnp.dot(
        lax.all_to_all(split_view, "frames", split_axis=2, concat_axis=0, tiled=True),
        temporal_weight,
        preferred_element_type=F32,
    ).astype(BF16)
    spread_out = temporal_mix(
        projected[..., :width],
        projected[..., width : 2 * width],
        projected[..., 2 * width :],
        time_scale,
    )
    returned = lax.all_to_all(spread_out, "frames", split_axis=0, concat_axis=2, tiled=True)
    mixed_time = returned.reshape(latents.shape)
    third = second + jnp.dot(mixed_time, temporal_out, preferred_element_type=F32)
    normed_three = layer_norm(third, norm_gains[2])
    both = jnp.dot(normed_three, ff_in, preferred_element_type=F32)
    half = ff_out.shape[0]
    ff_hidden = (both[..., :half] * jax.nn.gelu(both[..., half:], approximate=False)).astype(BF16)
    return third + jnp.dot(ff_hidden, ff_out, preferred_element_type=F32)


def solution(mesh):
    split = P("frames", "rows", None, None)
    return jax.shard_map(
        body,
        mesh=mesh,
        in_specs=(split,) * 3 + (P(),) * 9,
        out_specs=split,
        check_vma=False,
    )
```

time: 683 us -> 165 us (0.24)
  local copies, waits for them, and re-layouts: 341 us -> 28.8 us
  waiting for transfers between devices: 173 us -> 0.01 us
  Pallas kernels: 0 us -> 74.4 us
  matrix products: 102 us -> 32.7 us
  other arithmetic: 19.2 us -> 3.08 us
  between operations: 13.8 us -> 0.39 us
    reshape x30 -> x1, local copies, waits for them, and re-layouts: 231 us -> 1.57 us  [temporal_mix(): return mixed.astype(BF16).reshape(shape)]
    all_gather x2 -> x0, waiting for transfers between devices: 168 us -> none  [the longest x1 88.5 us: body(): lax.all_gather(stale_keys, 'rows', axis=1, tiled=True)]
    dynamic_slice x16 -> x0, local copies, waits for them, and re-layouts: 83.5 us -> none  [scan_rows(): lax.scan(visit, state, (jnp.arange(count, dtype=jnp.int32),) + stacked)]
    dot_general x25 -> x6, matrix products: 89.7 us -> 14.9 us  [the longest x1 5.73 us: body(): return third + jnp.dot(ff_hidden, ff_out, preferred_element_type=F32)]
    pallas_call x0 -> x1, Pallas kernels: none -> 74.4 us  [spatial(): pl.pallas_call(spatial_kernel, out_shape=jax.ShapeDtypeStruct((2, 2, PATC...]
    reduce_sum x9 -> x0, other arithmetic: 14.1 us -> none  [attend_block(): total = total * factor + jnp.sum(weights, axis=-1)]
    unnamed x24, local copies, waits for them, and re-layouts: 1.88 us -> 10.3 us
  transfers between devices with their start and end apart: 4 -> 2, of which waited for: 3 -> 0; matrix products, arithmetic and copies ran while one was open for 10% -> 9% of each run, Pallas kernels for 0% -> 0%
where the time goes in v1:
time: 165 us; the launch traced here: 164 us
  Pallas kernels  74.4 us (45%)
  matrix products  32.7 us (20%)
  local copies, waits for them, and re-layouts  28.8 us (17%)
  blocking collectives  20.2 us (12%)
  starting transfers between devices  4.97 us (3%)
  other arithmetic  3.08 us (2%)
    pallas_call x1, Pallas kernels, spatial(): pl.pallas_call(spatial_kernel, out_shape=jax.ShapeDtypeStruct((2, 2, PATC...  74.4 us
    dot_general x9, matrix products, body(): jnp.dot(window, conv_weight[row_step * 3 + col_step], preferred_element_t...  14.4 us
    all_to_all x1, blocking collectives, body(): lax.all_to_all(split_view, 'frames', split_axis=2, concat_axis=0, tiled=T...  11.2 us
    unnamed x24, local copies, waits for them, and re-layouts  10.3 us
    all_to_all x1, blocking collectives, body(): lax.all_to_all(spread_out, 'frames', split_axis=0, concat_axis=2, tiled=T...  8.97 us
    dot_general x1, matrix products, body(): return third + jnp.dot(ff_hidden, ff_out, preferred_element_type=F32)  5.73 us
    dot_general x1, matrix products, body(): both = jnp.dot(normed_three, ff_in, preferred_element_type=F32)  4.61 us
    transpose x2, local copies, waits for them, and re-layouts, half_columns(): return jnp.transpose(split, (2, 0, 1, 3)).reshape(2, 640, count * HALF)  3.82 us
  transfers between devices with their start and end apart: 2, of which 0 were waited for; matrix products, arithmetic and copies ran while one was open for 9% of the time, Pallas kernels for 0%

profile of v1, /device:TPU:0, one launch (start us, length us, event | category | flops | bytes accessed | tf_op | source)
XLA Modules:
  0.0 164.5 jit_solution(3013902955808898115)
XLA Ops:
  0.0 1.8 %fusion.146 = (bf16[2,1,48,640]{3,2,1,0:T(8,128)(2,1)}, bf16[2,1,48,640]{3,2,1,0:T(8,128)(2,1)}) fusion(bf16[2,2,48,640]{3,2,1,0:T(8,128)(2,1)} %param.13), kind=kLoop, calls=%fused_computation.184 | loop fusion | bytes 491520 | tf_op jit(solution)/shard_map/slice | solution.py:30
  1.8 1.3 collective-permute-start.1
  3.1 3.7 %collective-permute-start = (bf16[2,1,48,640]{3,2,1,0:T(8,128)(2,1)}, bf16[2,1,48,640]{3,2,1,0:T(8,128)(2,1)}, u32[]{:S(2)}, u32[]{:S(2)}) collective-permute-start(bf16[2,1,48,640]{3,2,1,0:T(8,128)(2,1)} %get-tuple-element.13), channel_id=1, source_target_pairs={{0,2},{2,4},{4,6},{6,8},{8,10},{10,12},{12,14},{14,16},{16,18},{18... | collective-permute-start | bytes 368648 | tf_op jit(solution)/shard_map/ppermute | solution.py:33
  6.8 4.3 %copy.32 = bf16[640,1920]{0,1:T(8,128)(2,1)} copy(bf16[640,1920]{1,0:T(8,128)(2,1)} %param.18) | data formatting | bytes 4915200 | tf_op args[6]
  11.1 1.9 %pad_bitcast_fusion = bf16[2,640,3,384]{1,3,0,2:T(8,128)(2,1)S(1)} fusion(bf16[640,3,2,320]{0,3,2,1:T(8,128)(2,1)} %bitcast.155), kind=kLoop, calls=%fused_computation.6 | loop fusion | bytes 5406720 | tf_op jit(solution)/shard_map/transpose | solution.py:366
  13.1 1.9 %copy.33 = bf16[2,640,3,384]{1,3,2,0:T(8,128)(2,1)} copy(bf16[2,640,3,384]{1,3,0,2:T(8,128)(2,1)S(1)} %pad_bitcast_fusion) | data formatting | bytes 5898240 | tf_op jit(solution)/shard_map/transpose | solution.py:366
  15.0 0.1 mul.116
  15.0 0.1 broadcast_in_dim.4
  15.1 0.1 broadcast_in_dim.5
  15.2 3.0 %slice.146 = bf16[2,640,768]{1,2,0:T(8,128)(2,1)} slice(bf16[2,640,1152]{1,2,0:T(8,128)(2,1)} %bitcast.153), slice={[0:2], [0:640], [384:1152]} | slice | bytes 3932160 | tf_op jit(solution)/shard_map/slice | solution.py:404
  18.3 4.1 %copy.64.w_ref = bf16[2,640,768]{2,1,0:T(8,128)(2,1)} copy(bf16[2,640,768]{1,2,0:T(8,128)(2,1)} %slice.146) | data formatting | bytes 3932160
  22.4 1.3 fusion.33
  23.6 1.5 fusion.66
  25.2 1.5 fusion.69
  26.7 1.5 fusion.71
  28.3 1.5 fusion.74
  29.8 1.5 fusion.76
  31.4 1.5 fusion.79
  32.9 1.7 %fusion.22 = f32[2,2,48,640]{3,2,1,0:T(8,128)S(1)} fusion(f32[2,2,48,640]{3,2,1,0:T(8,128)S(1)} %fusion.74, f32[2,2,48,640]{3,2,1,0:T(8,128)S(1)} %fusion.76, f32[2,2,48,640]{3,2,1,0:T(8,128)S(1)} %fusion.79, bf16[9,640,640]{2,1,0:T(8,128)(2,1)} %param.17, bf16[2,1,48,640]{3,2,1,0:T(8,128)(2,1)} %collective-permute-done.1, ...), kind=kOutput, calls=%fused_computation.39 | convolution fusion | flops 160358400 | bytes 3276800 | tf_op jit(solution)/shard_map/dot_general | solution.py:392
  34.6 1.6 fusion.24
  36.2 1.9 %fusion.147 = (f32[2,2,48]{2,1,0:T(2,128)S(1)}, f32[2,2,48,640]{3,2,1,0:T(8,128)S(1)}) fusion(f32[2,2,48,640]{3,2,1,0:T(8,128)S(1)} %fusion.66, f32[2,2,48,640]{3,2,1,0:T(8,128)S(1)} %fusion.24, bf16[9,640,640]{2,1,0:T(8,128)(2,1)} %param.17, bf16[2,1,48,640]{3,2,1,0:T(8,128)(2,1)} %collective-permute-done.1, bf16[2,2,48,640]{3,2,1,0:T(8,128)(2,1)S(1)} %copy-done.7, ...), kind=kOutput, calls=%fused_computation.185 | convolution fusion | flops 160603968 | bytes 3031808 | tf_op jit(solution)/shard_map/dot_general | solution.py:392
  38.1 0.2 multiply_reduce_fusion.2
  38.3 0.1 multiply_convert_fusion.2
  38.5 0.0 copy-start.2
  38.5 1.1 convolution_bitcast_fusion
  39.6 0.1 slice.213.kv_ref
  39.7 1.4 copy-done.1
  41.1 74.4 %spatial.1 = bf16[2,2,96,384]{3,2,1,0:T(8,128)(2,1)S(1)} custom-call(bf16[2,96,640]{2,1,0:T(8,128)(2,1)S(1)} %bitcast.152, bf16[2,2,96,384]{3,2,1,0:T(8,128)(2,1)S(1)} %fusion.92.q_ref, bf16[2,2,96,768]{3,2,1,0:T(8,128)(2,1)S(1)} %slice.213.kv_ref, bf16[2,640,768]{2,1,0:T(8,128)(2,1)S(1)} %copy-done.1), custom_call_target="tpu_custom_call" | custom-call | tf_op jit(solution)/shard_map/spatial/pallas_call | solution.py:329
  115.6 0.5 fusion.148
  116.1 0.2 multiply_reduce_fusion.1
  116.3 0.5 copy-done.4
  116.9 0.1 multiply_convert_fusion.1
  117.0 11.2 %all_to_all.30 = bf16[2,2,2,24,640]{4,3,1,0,2:T(8,128)(2,1)S(1)} all-to-all(bf16[2,2,2,24,640]{4,3,1,0,2:T(8,128)(2,1)S(1)} %copy.37), channel_id=1, replica_groups=mesh['rows'=64,'frames'=2] {'frames'}, dimensions={2} | all-to-all | bytes 491520 | tf_op jit(solution)/shard_map/all_to_all | solution.py:414
  128.3 0.8 fusion.5
  129.1 0.9 fusion.144
  130.0 2.3 %reshape.104 = bf16[4,48,10,64]{3,2,1,0:T(8,128)(2,1)} reshape(bf16[4,2,1,24,640]{4,3,1,0,2:T(8,128)(2,1)} %get-tuple-element.9) | data formatting | bytes 491520 | tf_op jit(solution)/shard_map/reshape | solution.py:51
  132.2 2.3 %reshape.103 = bf16[4,48,10,64]{3,2,1,0:T(8,128)(2,1)} reshape(bf16[4,2,1,24,640]{4,3,1,0,2:T(8,128)(2,1)} %get-tuple-element.10) | data formatting | bytes 491520 | tf_op jit(solution)/shard_map/reshape | solution.py:50
  134.5 1.3 reshape.102
  135.8 2.6 %fusion.149 = (f32[48,10,4]{2,1,0:T(8,128)S(1)}, f32[48,10,4,4]{2,3,1,0:T(4,128)S(1)}) fusion(f32[10]{0:T(128)S(1)} %get-tuple-element.15, bf16[4,48,10,64]{3,2,1,0:T(8,128)(2,1)} %reshape.104, bf16[4,48,10,64]{3,2,1,0:T(8,128)(2,1)} %reshape.103), kind=kOutput, calls=%fused_computation.187 | convolution fusion | flops 996480 | bytes 529960 | tf_op jit(solution)/shard_map/anhd,bnhd->nhab/dot_general | solution.py:54
  138.4 0.9 fusion.90
  139.3 1.3 fusion.20
  140.5 1.0 copy.42
  141.6 1.6 reshape.105
  143.1 9.0 %all_to_all.31 = bf16[4,2,1,24,640]{4,3,1,2,0:T(8,128)(2,1)S(1)} all-to-all(bf16[4,2,1,24,640]{4,3,1,2,0:T(8,128)(2,1)S(1)} %bitcast.160), channel_id=1, replica_groups=mesh['rows'=64,'frames'=2] {'frames'}, dimensions={0} | all-to-all | bytes 491520 | tf_op jit(solution)/shard_map/all_to_all | solution.py:424
  152.1 1.8 %fusion.150 = (f32[2,2,48]{2,1,0:T(2,128)S(1)}, f32[2,2,48,640]{3,2,1,0:T(8,128)S(1)}) fusion(f32[2,2,48,640]{3,2,1,0:T(8,128)} %copy-done.4, bf16[2,2,48,640]{3,2,1,0:T(8,128)(2,1)S(1)} %bitcast.157, bf16[640,640]{1,0:T(8,128)(2,1)} %param.21), kind=kOutput, calls=%fused_computation.188 | convolution fusion | flops 157531968 | bytes 2048768 | tf_op jit(solution)/shard_map/dot_general | solution.py:426
  153.9 0.2 multiply_reduce_fusion
  154.1 4.6 %fusion = f32[2,2,48,5120]{3,2,1,0:T(8,128)S(1)} fusion(bf16[640,5120]{1,0:T(8,128)(2,1)} %param.22, f32[2,2,48,640]{3,2,1,0:T(8,128)S(1)} %get-tuple-element.24, f32[640]{0:T(1024)S(1)} %get-tuple-element.5, f32[2,2,48]{2,1,0:T(2,128)S(1)} %add_rsqrt_fusion, f32[2,2,48]{2,1,0:T(2,128)S(1)} %broadcast_multiply_fusion), kind=kOutput, calls=%fused_computation | convolution fusion | flops 1258782720 | bytes 10981376 | tf_op jit(solution)/shard_map/dot_general | solution.py:428
  158.7 5.7 %fusion.27 = f32[2,2,48,640]{3,2,1,0:T(8,128)} fusion(f32[2,2,48,640]{3,2,1,0:T(8,128)S(1)} %get-tuple-element.24, bf16[2560,640]{1,0:T(8,128)(2,1)S(1)} %copy-done, f32[2,2,48,5120]{3,2,1,0:T(8,128)S(1)} %fusion), kind=kOutput, calls=%fused_computation.46 | convolution fusion | flops 661708800 | bytes 8192000 | tf_op jit(solution)/shard_map/dot_general | solution.py:431
  (34 shorter events, 0.3 us)
Async XLA Ops:
  0.0 158.7 %copy-start = (bf16[2560,640]{1,0:T(8,128)(2,1)S(1)}, bf16[2560,640]{1,0:T(8,128)(2,1)}, u32[]{:S(2)}) copy-start(bf16[2560,640]{1,0:T(8,128)(2,1)} %param.23) | copy-start | bytes 9830404
  1.8 20.5 %collective-permute-start.1 = (bf16[2,1,48,640]{3,2,1,0:T(8,128)(2,1)}, bf16[2,1,48,640]{3,2,1,0:T(8,128)(2,1)}, u32[]{:S(2)}, u32[]{:S(2)}) collective-permute-start(bf16[2,1,48,640]{3,2,1,0:T(8,128)(2,1)} %get-tuple-element.14), channel_id=1, source_target_pairs={{2,0},{4,2},{6,4},{8,6},{10,8},{12,10},{14,12},{16,14},{18,16},{20... | collective-permute-start | bytes 368648 | tf_op jit(solution)/shard_map/ppermute | solution.py:35
  3.1 8.0 %copy-start.9 = (f32[2,10]{1,0:T(2,128)S(1)}, f32[2,10]{1,0:T(2,128)}, u32[]{:S(2)}) copy-start(f32[2,10]{1,0:T(2,128)} %param.16) | copy-start | bytes 244
  3.1 19.2 %collective-permute-start = (bf16[2,1,48,640]{3,2,1,0:T(8,128)(2,1)}, bf16[2,1,48,640]{3,2,1,0:T(8,128)(2,1)}, u32[]{:S(2)}, u32[]{:S(2)}) collective-permute-start(bf16[2,1,48,640]{3,2,1,0:T(8,128)(2,1)} %get-tuple-element.13), channel_id=1, source_target_pairs={{0,2},{2,4},{4,6},{6,8},{8,10},{10,12},{12,14},{14,16},{16,18},{18... | collective-permute-start | bytes 368648 | tf_op jit(solution)/shard_map/ppermute | solution.py:33
  18.2 4.1 %copy-start.8 = (f32[3,640]{1,0:T(4,128)S(1)}, f32[3,640]{1,0:T(4,128)}, u32[]{:S(2)}) copy-start(f32[3,640]{1,0:T(4,128)} %param.15) | copy-start | bytes 23044
  18.2 4.1 %copy-start.7 = (bf16[2,2,48,640]{3,2,1,0:T(8,128)(2,1)S(1)}, bf16[2,2,48,640]{3,2,1,0:T(8,128)(2,1)}, u32[]{:S(2)}) copy-start(bf16[2,2,48,640]{3,2,1,0:T(8,128)(2,1)} %param.12) | copy-start | bytes 737284
  36.2 2.3 %copy-start.3 = (bf16[2,640,3,384]{1,3,2,0:T(8,128)(2,1)S(1)}, bf16[2,640,3,384]{1,3,2,0:T(8,128)(2,1)}, u32[]{:S(2)}) copy-start(bf16[2,640,3,384]{1,3,2,0:T(8,128)(2,1)} %copy.33) | copy-start | bytes 8847364
  38.5 1.2 copy-start.2
  39.6 1.5 copy-start.1
  41.1 74.5 %copy-start.5 = (bf16[640,640]{1,0:T(8,128)(2,1)S(1)}, bf16[640,640]{1,0:T(8,128)(2,1)}, u32[]{:S(2)}) copy-start(bf16[640,640]{1,0:T(8,128)(2,1)} %param.19) | copy-start | bytes 2457604
  115.6 12.7 %copy-start.10 = (bf16[640,1920]{1,0:T(8,128)(2,1)S(1)}, bf16[640,1920]{1,0:T(8,128)(2,1)}, u32[]{:S(2)}) copy-start(bf16[640,1920]{1,0:T(8,128)(2,1)} %param.20) | copy-start | bytes 7372804
  116.1 0.8 copy-start.4
  135.8 3.5 %copy-start.6 = (bf16[4,48,10,64]{3,2,1,0:T(8,128)(2,1)S(1)}, bf16[4,48,10,64]{3,2,1,0:T(8,128)(2,1)}, u32[]{:S(2)}) copy-start(bf16[4,48,10,64]{3,2,1,0:T(8,128)(2,1)} %reshape.102) | copy-start | bytes 737284

commit v2 on v1

v2 whole, which is shorter than its diff:
```python
import functools
import math

import jax
import jax.numpy as jnp
from jax import lax
from jax.experimental import pallas as pl
from jax.experimental.pallas import tpu as pltpu
from jax.sharding import PartitionSpec as P

HEAD_DIM = 64
NEG = -1e30
EPS = 1e-05
F32 = jnp.float32
BF16 = jnp.bfloat16
MESH = pl.DeviceIdType.MESH
NT = (((1,), (1,)), ((), ()))
WIDTH = 640
COLS = 48
PATCH = 96
QUERIES = 384
HALF = 384
HIDDEN = 2560
FF_STEP = 512
LOG2E = math.log2(math.e)

SLOTS = {
    (1, 0): (0, 0), (3, 0): (0, 1), (0, 1): (0, 2), (0, 3): (0, 3),
    (1, 1): (1, 0), (1, 3): (1, 1), (3, 1): (1, 2), (3, 3): (1, 3),
    (2, 1): (2, 0), (2, 3): (2, 1), (1, 2): (2, 2), (3, 2): (2, 3),
    (0, 0): (3, 0), (2, 0): (3, 1), (0, 2): (3, 2), (2, 2): (3, 3),
}


def dot(left, right):
    return jnp.dot(left, right, preferred_element_type=F32)


def layer_norm(values, gain):
    centre = values - jnp.mean(values, axis=-1, keepdims=True)
    spread = jnp.mean(centre * centre, axis=-1, keepdims=True)
    return (centre * lax.rsqrt(spread + EPS) * gain).astype(BF16)


def block_kernel(
    latents_hbm, previous_hbm, stale_hbm, gains_ref, scale_ref, conv_hbm, attn_hbm, attn_out_hbm,
    time_hbm, time_out_hbm, ff_in_hbm, ff_out_hbm,
    out_ref,
    lat, halo, field, conv_w, wall, attn_out_w, time_w, time_out_w, ff_in_w, ff_out_w,
    first, first_all, q_now, kv_now, xall, q_in, kv_in, q_heads, kv, acc, peak, total,
    result, mixes, time_qkv, time_mix, third, hidden, back, back_in,
    load, recv, sent, q_recv, q_sent, kv_recv, kv_sent, r_recv, r_sent, h_recv, h_sent,
    f_recv, f_sent, local,
):
    row = lax.axis_index("rows")
    part = lax.axis_index("frames")
    core = row % 2
    z = (row // 2) % 4
    y = (row // 8) % 2
    x = row // 16

    def device(x, y, z, core, part=part):
        return (((x * 2 + y) * 4 + z) * 2 + core, part)

    def ring(along_first, step):
        dx = step * (1 - core) if along_first else step * core
        dz = step * core if along_first else step * (1 - core)
        return device((x + dx + 4) % 4, y, (z + dz + 4) % 4, core)

    a_up, a_down = ring(True, 1), ring(True, -1)
    b_up, b_down = ring(False, 1), ring(False, -1)

    def column(dc, dy, part):
        return device(x, (y + dy) % 2, z, (core + dc) % 2, part)

    mate, across = column(1, 0, part), column(0, 1, part)
    quad = [(0, 1, across), (1, 0, mate), (1, 1, column(1, 1, part))]
    partner = (row, 1 - part)

    loads = []

    def fetch(src, dst):
        copy = pltpu.make_async_copy(src, dst, load.at[len(loads)])
        loads.append(copy)
        copy.start()
        return copy

    lat_copy = fetch(latents_hbm, lat)
    conv_copies = [
        fetch(conv_hbm.at[pl.ds(3 * tap, 3)], conv_w.at[pl.ds(3 * tap, 3)]) for tap in (1, 0, 2)
    ]

    barrier = pltpu.get_barrier_semaphore()

    def greet(other):
        pl.semaphore_signal(barrier, inc=1, device_id=other, device_id_type=MESH)

    for other in (a_up, a_down, b_up, b_down) + tuple(item[2] for item in quad):
        greet(other)
    for dc in range(2):
        for dy in range(2):
            greet(column(dc, dy, 1 - part))

    @pl.when(row > 0)
    def _():
        greet((row - 1, part))

    @pl.when(row < 63)
    def _():
        greet((row + 1, part))

    wall_copies = []
    for half in range(2):
        for kind in range(3):
            wall_copies.append(fetch(
                attn_hbm.at[:, pl.ds(WIDTH * kind + 384 * half, 256)],
                wall.at[half, :, pl.ds(HALF * kind, 256)],
            ))
            wall_copies.append(fetch(
                attn_hbm.at[:, pl.ds(WIDTH * kind + 256, 128)],
                wall.at[half, :, pl.ds(HALF * kind + 256, 128)],
            ))
    late_copies = [
        fetch(attn_out_hbm, attn_out_w), fetch(time_hbm, time_w), fetch(time_out_hbm, time_out_w),
        fetch(ff_in_hbm, ff_in_w), fetch(ff_out_hbm, ff_out_w),
    ]

    @pl.when((row > 0) & (row < 63))
    def _():
        pl.semaphore_wait(barrier, 13)

    @pl.when((row == 0) | (row == 63))
    def _():
        pl.semaphore_wait(barrier, 12)

    started = []

    def remote(src, dst, send_sem, recv_sem, to):
        return pltpu.make_async_remote_copy(
            src_ref=src, dst_ref=dst, send_sem=send_sem, recv_sem=recv_sem,
            device_id=to, device_id_type=MESH,
        )

    to_above = remote(previous_hbm.at[:, 0], halo.at[1], h_sent.at[0], h_recv.at[1], (row - 1, part))
    to_below = remote(previous_hbm.at[:, 1], halo.at[0], h_sent.at[1], h_recv.at[0], (row + 1, part))

    @pl.when(row > 0)
    def _():
        to_above.start()

    @pl.when(row < 63)
    def _():
        to_below.start()

    def send(src, at, to, dc=0, dy=None, places=1):
        group, place = SLOTS[at]
        if dy is not None:
            dst = xall.at[group, dc, place, dy]
        else:
            dst = xall.at[group, dc, pl.ds(place, places)]
        copy = remote(
            src, dst, sent.at[len(started)], recv.at[group, dc, place, dy or 0], to
        )
        started.append(copy)
        return copy

    def arrival(at, dc=0, dy=None, places=1):
        group, place = SLOTS[at]
        if dy is not None:
            dst = xall.at[group, dc, place, dy]
        else:
            dst = xall.at[group, dc, pl.ds(place, places)]
        sem = recv.at[group, dc, place, dy or 0]
        return lambda: remote(dst, dst, sem, sem, mate).wait_recv()

    def held(at, dy=None, places=1):
        group, place = SLOTS[at]
        if dy is not None:
            return xall.at[group, 0, place, dy]
        return xall.at[group, 0, pl.ds(place, places)]

    def arrive(at, dc=0, dy=None, places=1):
        arrival(at, dc, dy, places)()

    def own_ways(src, dy):
        return [
            send(src, (3, 0), a_up, dy=dy), send(src, (1, 0), a_down, dy=dy),
            send(src, (0, 3), b_up, dy=dy), send(src, (0, 1), b_down, dy=dy),
            send(src, (0, 0), mate, dc=1, dy=dy),
        ]

    def start(copies):
        for copy in copies:
            copy.start()

    own = stale_hbm.at[y]
    start([send(stale_hbm.at[1 - y], (0, 0), across, dy=1)])
    start(own_ways(own, 0))
    keep_own = pltpu.make_async_copy(own, held((0, 0), 0), local.at[0])
    keep_own.start()

    neighbours_a = [
        send(held((3, 0), 0), (2, 0), a_up, dy=0), send(held((1, 0), 1), (2, 0), a_down, dy=1),
        send(held((1, 0)), (1, 3), b_up), send(held((1, 0)), (1, 1), b_down),
        send(held((3, 0)), (3, 3), b_up), send(held((3, 0)), (3, 1), b_down),
        send(held((1, 0), places=2), (1, 0), mate, dc=1, places=2),
    ]

    def along_b(da, places):
        copies = [
            send(held((da, 3), 0), (da, 2), b_up, dy=0),
            send(held((da, 1), 1), (da, 2), b_down, dy=1),
        ]
        return copies + [send(held((da, 1), places=2), (da, 1), mate, dc=1, places=2)]

    on_b = {da: along_b(da, 2) for da in range(4)}
    far_a = [
        send(held((2, 0)), (2, 3), b_up), send(held((2, 0)), (2, 1), b_down),
        send(held((2, 0)), (2, 0), mate, dc=1),
    ]
    far_b = [send(held((0, 2)), (0, 2), mate, dc=1)]
    far_lines = [send(held((1, 2), places=2), (1, 2), mate, dc=1, places=2)]
    corner = [send(held((2, 2)), (2, 2), mate, dc=1)]
    dy_ways = own_ways(held((0, 0), 1), 1)

    def own_second():
        arrive((0, 0), dy=1)
        start(dy_ways)

    def near():
        for dy in range(2):
            arrive((1, 0), dy=dy)
            arrive((3, 0), dy=dy)
        start(neighbours_a)
        for dy in range(2):
            arrive((0, 1), dy=dy)
            arrive((0, 3), dy=dy)
        start(on_b[0])

    def far_first():
        for dy in range(2):
            arrive((2, 0), dy=dy)
        start(far_a)

    def far_second():
        for dy in range(2):
            arrive((0, 2), dy=dy)
        start(far_b)

    def line(da):
        arrive((da, 1))
        arrive((da, 3))
        start(on_b[da])

    def lines_far():
        for da in (1, 3):
            for dy in range(2):
                arrive((da, 2), dy=dy)
        start(far_lines)

    def last_corner():
        for dy in range(2):
            arrive((2, 2), dy=dy)
        start(corner)

    column_at = lax.broadcasted_iota(jnp.int32, (COLS, WIDTH), 0)

    def fill(at, values):
        for frame in range(2):
            cells = values[frame].astype(F32)
            cells = cells * (1.0 / (1.0 + jnp.exp(-cells)))
            left = jnp.where(column_at == 0, 0.0, pltpu.roll(cells, 1, 0))
            right = jnp.where(column_at == COLS - 1, 0.0, pltpu.roll(cells, COLS - 1, 0))
            field[frame, at, :, :WIDTH] = left.astype(BF16)
            field[frame, at, :, WIDTH : 2 * WIDTH] = cells.astype(BF16)
            field[frame, at, :, 2 * WIDTH :] = right.astype(BF16)

    def taps(at):
        return dot(
            field[:, at : at + 2].reshape(2 * PATCH, 3 * WIDTH),
            conv_w[3 * at : 3 * at + 3].reshape(3 * WIDTH, WIDTH),
        )

    lat_copy.wait()
    fill(1, lat[:, 0])
    fill(2, lat[:, 1])
    conv_copies[0].wait()
    conv_sum = taps(1)
    own_second()

    @pl.when(row > 0)
    def _():
        to_below.wait_recv()

    @pl.when(row == 0)
    def _():
        halo[0] = jnp.zeros_like(halo[0])

    @pl.when(row < 63)
    def _():
        to_above.wait_recv()

    @pl.when(row == 63)
    def _():
        halo[1] = jnp.zeros_like(halo[1])

    fill(0, halo[0])
    fill(3, halo[1])
    conv_copies[1].wait()
    conv_sum = conv_sum + taps(0)
    conv_copies[2].wait()
    conv_sum = conv_sum + taps(2)
    start_sum = lat[...].reshape(2 * PATCH, WIDTH).astype(F32) + conv_sum
    parts = start_sum.reshape(2, 2, COLS, WIDTH)
    first[0] = parts[:, 0]
    first[1] = parts[:, 1]
    first_copy = remote(
        first.at[1 - part], first_all.at[part], f_sent.at[0], f_recv.at[0], partner
    )
    first_copy.start()
    normed = layer_norm(start_sum, gains_ref[0:1, :])
    for copy in wall_copies:
        copy.wait()
    lane = lax.broadcasted_iota(jnp.int32, (QUERIES, 128), 1)
    half_lane = lax.broadcasted_iota(jnp.int32, (1, 128), 1) // HEAD_DIM

    def lane_scale(kind, pair):
        low, high = scale_ref[kind, 2 * pair], scale_ref[kind, 2 * pair + 1]
        return jnp.where(half_lane == 0, low, high) * (LOG2E / math.sqrt(HEAD_DIM))

    for half in range(2):
        triple = dot(normed, wall[half]).reshape(2, PATCH, 3 * HALF)
        for place, pair in enumerate((3 * half, 3 * half + 1, 2)):
            lanes = slice(128 * place, 128 * place + 128)
            q_now[:, half, :, lanes] = (triple[..., lanes] * lane_scale(0, pair)).astype(BF16)
        kv_now[:, half] = triple[..., HALF:].astype(BF16)
    q_copies, kv_copies = [], []
    for dc, dy, to in quad:
        at = dc * 2 + dy
        q_copies.append(remote(
            q_now.at[(y + dy) % 2, (core + dc) % 2], q_in.at[at], q_sent.at[at], q_recv.at[at], to
        ))
        kv_copies.append(remote(
            kv_now.at[(y + dy) % 2, (core + dc) % 2], kv_in.at[at], kv_sent.at[at],
            kv_recv.at[at], to,
        ))
    start(q_copies)
    start(kv_copies)
    q_in[0] = q_now[y, core]
    kv_in[0] = kv_now[y, core]
    near()
    keep_own.wait()
    arrive((0, 0), dc=1, dy=0)
    arrive((0, 0), dc=1, dy=1)

    def project(rows, at):
        count = rows.shape[0] * rows.shape[1] * rows.shape[2] * rows.shape[3]
        kv[at : at + count] = dot(
            rows.reshape(count, WIDTH), wall[core, :, HALF:]
        ).astype(BF16)

    for dc in range(2):
        project(xall[3, dc, 0:1], dc * 2 * PATCH)

    for copy in q_copies:
        copy.wait_recv()
    for pair in range(3):
        both = q_in[:, :, 128 * pair : 128 * pair + 128].reshape(QUERIES, 128)
        zero = jnp.zeros_like(both)
        if pair < 2:
            q_heads[2 * pair] = jnp.where(lane < HEAD_DIM, both, zero)
            q_heads[2 * pair + 1] = jnp.where(lane < HEAD_DIM, zero, both)
        else:
            q_heads[4] = jnp.where(lane // HEAD_DIM == core, both, zero)
    acc[...] = jnp.zeros_like(acc)
    total[...] = jnp.zeros_like(total)
    peak[...] = jnp.full_like(peak, NEG)

    def attend(keys, masked, hooks):
        for pair in range(3):
            k = kv[:keys, 128 * pair : 128 * pair + 128]
            v = kv[:keys, HALF + 128 * pair : HALF + 128 * pair + 128]
            factors, sums = [], []
            for head in range(2 * pair, min(2 * pair + 2, 5)):
                s = lax.dot_general(q_heads[head], k, NT, preferred_element_type=F32)
                if masked:
                    q_patch = lax.broadcasted_iota(jnp.int32, (QUERIES, keys), 0) // PATCH
                    k_patch = lax.broadcasted_iota(jnp.int32, (QUERIES, keys), 1) // PATCH
                    drop = ((k_patch < 4) & (k_patch == q_patch)) | (
                        (k_patch >= 4) & (k_patch != q_patch + 4)
                    )
                    s = jnp.where(drop, NEG, s)
                old = peak[head]
                new = jnp.maximum(old, jnp.max(s, axis=1, keepdims=True))
                factor = jnp.exp2(old - new)
                w = jnp.exp2(s - new[:, :1])
                total[head] = total[head] * factor + jnp.sum(w, axis=1, keepdims=True)
                peak[head] = new
                factors.append(factor)
                sums.append(dot(w.astype(BF16), v))
                if head in hooks:
                    hooks[head]()
            if len(sums) == 2:
                acc[pair] = acc[pair] * jnp.where(lane < HEAD_DIM, *factors) + jnp.where(
                    lane < HEAD_DIM, *sums
                )
            else:
                acc[pair] = acc[pair] * factors[0] + sums[0]

    for copy in kv_copies:
        copy.wait_recv()
    kv[4 * PATCH : 8 * PATCH] = kv_in[...].reshape(4 * PATCH, 2 * HALF)
    attend(8 * PATCH, True, {2: far_first})

    def group(g, carry):
        def when(table):
            def hook():
                for at, actions in table.items():
                    @pl.when(g == at)
                    def _():
                        for action in actions:
                            action()
            return hook

        when({
            0: [arrival((1, 0), 1, None, 2), arrival((0, 1), 1, None, 2)],
            1: [arrival((1, 1), 1, None, 2), arrival((3, 1), 1, None, 2)],
            2: [arrival((2, 1), 1, None, 2), arrival((1, 2), 1, None, 2)],
        })()
        for dc in range(2):
            project(xall[g, dc], dc * 8 * PATCH)
        attend(16 * PATCH, False, {
            0: when({0: [functools.partial(line, 1)]}),
            1: when({0: [functools.partial(line, 3)]}),
            2: when({0: [far_second], 1: [functools.partial(line, 2)], 2: [last_corner]}),
            4: when({1: [lines_far]}),
        })
        return carry

    lax.fori_loop(0, 3, group, 0)
    arrive((2, 0), 1)
    arrive((0, 2), 1)
    arrive((2, 2), 1)
    for dc in range(2):
        project(xall[3, dc, 1:4], dc * 6 * PATCH)
    attend(12 * PATCH, False, {})

    for pair in range(3):
        below = total[2 * pair]
        if pair < 2:
            below = jnp.where(lane < HEAD_DIM, below, total[2 * pair + 1])
        mixed = acc[pair] / below
        if pair == 2:
            mixed = jnp.where(lane // HEAD_DIM == core, mixed, 0.0)
        result[:, :, :, 128 * pair : 128 * pair + 128] = mixed.astype(BF16).reshape(4, 2, COLS, 128)
    r_copies = []
    for flip in (1, 0):
        for dc in range(2):
            for dy in range(2):
                if flip + dc + dy == 0:
                    continue
                to_part = part + flip - 2 * part * flip
                at = 4 * flip + 2 * dc + dy
                r_copies.append(remote(
                    result.at[2 * dc + dy, to_part], mixes.at[2 * part + y, core],
                    r_sent.at[at], r_recv.at[at], column(dc, dy, to_part),
                ))
    start(r_copies)
    mixes[2 * part + y, core] = result[0, part]
    first_all[part] = first[part]
    first_copy.wait_recv()
    for copy in late_copies:
        copy.wait()
    for copy in r_copies:
        copy.wait_recv()

    rows = 4 * COLS
    middle = mixes[:, 0, :, 256:] + mixes[:, 1, :, 256:]
    mix = jnp.concatenate(
        [mixes[:, 0, :, :256], middle, mixes[:, 1, :, :256]], axis=-1
    ).reshape(rows, WIDTH)
    second = first_all[...].reshape(rows, WIDTH) + dot(mix, attn_out_w[...])
    third[...] = second
    time_qkv[...] = dot(layer_norm(second, gains_ref[1:2, :]), time_w[...]).astype(BF16)

    ones_row = lax.broadcasted_iota(jnp.int32, (256, 128), 0) % 128 // HEAD_DIM
    ones_col = lax.broadcasted_iota(jnp.int32, (256, 128), 1) // HEAD_DIM
    ones = jnp.where(ones_row == ones_col, 1.0, 0.0).astype(BF16)
    for pair in range(5):
        def lanes_of(kind):
            at = WIDTH * kind + 128 * pair
            return time_qkv[:, at : at + 128].reshape(4, COLS, 128).astype(F32)

        tq, tk, tv = lanes_of(0), lanes_of(1), lanes_of(2)
        products = (tq[:, None] * tk[None]).reshape(16 * COLS, 128)
        high = products.astype(BF16)
        low = (products - high.astype(F32)).astype(BF16)
        s = dot(jnp.concatenate([high, low], axis=1), ones) * lane_scale(1, pair)
        s = s.reshape(4, 4, COLS, 128)
        w = jnp.exp2(s - jnp.max(s, axis=1, keepdims=True))
        mixed = jnp.sum(w.astype(BF16).astype(F32) * tv[None], axis=1) / jnp.sum(w, axis=1)
        time_mix[:, 128 * pair : 128 * pair + 128] = mixed.astype(BF16).reshape(rows, 128)
    third[...] = third[...] + dot(time_mix[...], time_out_w[...])
    normed_three = layer_norm(third[...], gains_ref[2:3, :])
    for step in range(HIDDEN // FF_STEP):
        at = FF_STEP * step
        value = dot(normed_three, ff_in_w[:, at : at + FF_STEP])
        gate = dot(normed_three, ff_in_w[:, HIDDEN + at : HIDDEN + at + FF_STEP])
        gelu = 0.5 * gate * (1.0 + lax.erf(gate * math.sqrt(0.5)))
        hidden[:, at : at + FF_STEP] = (value * gelu).astype(BF16)
    done = third[...] + dot(hidden[...], ff_out_w[...])
    third[...] = done
    half_rows = 2 * COLS
    back[...] = third[pl.ds(pl.multiple_of((1 - part) * half_rows, half_rows), half_rows)].astype(BF16)
    back_copy = remote(back, back_in, f_sent.at[1], f_recv.at[1], partner)
    back_copy.start()
    mine = third[pl.ds(pl.multiple_of(part * half_rows, half_rows), half_rows)]
    out_ref[:, part] = mine.reshape(2, COLS, WIDTH)
    back_copy.wait_recv()
    out_ref[:, 1 - part] = back_in[...].astype(F32).reshape(2, COLS, WIDTH)
    for copy in started + q_copies + kv_copies + r_copies + [first_copy, back_copy]:
        copy.wait_send()

    @pl.when(row > 0)
    def _():
        to_above.wait_send()

    @pl.when(row < 63)
    def _():
        to_below.wait_send()


def body(*arrays):
    vmem = pl.BlockSpec(memory_space=pltpu.VMEM)
    hbm = pl.BlockSpec(memory_space=pl.ANY)
    dma = pltpu.SemaphoreType.DMA
    rows = 4 * COLS
    return pl.pallas_call(
        block_kernel,
        out_shape=jax.ShapeDtypeStruct((2, 2, COLS, WIDTH), F32),
        in_specs=[hbm] * 3 + [vmem, pl.BlockSpec(memory_space=pltpu.SMEM)] + [hbm] * 7,
        out_specs=vmem,
        scratch_shapes=[
            pltpu.VMEM((2, 2, COLS, WIDTH), BF16),
            pltpu.VMEM((2, 2, COLS, WIDTH), BF16),
            pltpu.VMEM((2, 4, COLS, 3 * WIDTH), BF16),
            pltpu.VMEM((9, WIDTH, WIDTH), BF16),
            pltpu.VMEM((2, WIDTH, 3 * HALF), BF16),
            pltpu.VMEM((WIDTH, WIDTH), BF16),
            pltpu.VMEM((WIDTH, 3 * WIDTH), BF16),
            pltpu.VMEM((WIDTH, WIDTH), BF16),
            pltpu.VMEM((WIDTH, 2 * HIDDEN), BF16),
            pltpu.VMEM((HIDDEN, WIDTH), BF16),
            pltpu.VMEM((2, 2, COLS, WIDTH), F32),
            pltpu.VMEM((2, 2, COLS, WIDTH), F32),
            pltpu.VMEM((2, 2, PATCH, HALF), BF16),
            pltpu.VMEM((2, 2, PATCH, 2 * HALF), BF16),
            pltpu.VMEM((4, 2, 4, 2, 2, COLS, WIDTH), BF16),
            pltpu.VMEM((4, PATCH, HALF), BF16),
            pltpu.VMEM((4, PATCH, 2 * HALF), BF16),
            pltpu.VMEM((5, QUERIES, 128), BF16),
            pltpu.VMEM((16 * PATCH, 2 * HALF), BF16),
            pltpu.VMEM((3, QUERIES, 128), F32),
            pltpu.VMEM((5, QUERIES, 128), F32),
            pltpu.VMEM((5, QUERIES, 128), F32),
            pltpu.VMEM((4, 2, COLS, HALF), BF16),
            pltpu.VMEM((4, 2, COLS, HALF), BF16),
            pltpu.VMEM((rows, 3 * WIDTH), BF16),
            pltpu.VMEM((rows, WIDTH), BF16),
            pltpu.VMEM((rows, WIDTH), F32),
            pltpu.VMEM((rows, HIDDEN), BF16),
            pltpu.VMEM((PATCH, WIDTH), BF16),
            pltpu.VMEM((PATCH, WIDTH), BF16),
            dma((21,)),
            dma((4, 2, 4, 2)),
            dma((36,)),
            dma((4,)),
            dma((4,)),
            dma((4,)),
            dma((4,)),
            dma((8,)),
            dma((8,)),
            dma((2,)),
            dma((2,)),
            dma((2,)),
            dma((2,)),
            dma((1,)),
        ],
        compiler_params=pltpu.CompilerParams(
            collective_id=0, has_side_effects=True, vmem_limit_bytes=62 << 20
        ),
        name="block",
    )(*arrays)


def solution(mesh):
    split = P("frames", "rows", None, None)
    return jax.shard_map(
        body,
        mesh=mesh,
        in_specs=(split,) * 3 + (P(),) * 9,
        out_specs=split,
        check_vma=False,
    )
```

time: 165 us -> 89.3 us (0.54)
  matrix products: 32.7 us -> 0 us
  local copies, waits for them, and re-layouts: 28.8 us -> 1.84 us
  blocking collectives: 20.2 us -> 0 us
  Pallas kernels: 74.4 us -> 85.7 us
  starting transfers between devices: 4.97 us -> 0 us
  other arithmetic: 3.08 us -> 0 us
    dot_general x17 -> x0, matrix products: 32.7 us -> none  [the longest x9 14.4 us: body(): jnp.dot(window, conv_weight[row_step * 3 + col_step], preferred_element_t...]
    all_to_all x2 -> x0, blocking collectives: 20.2 us -> none  [the longest x1 11.2 us: body(): lax.all_to_all(split_view, 'frames', split_axis=2, concat_axis=0, tiled=T...]
    pallas_call x1, Pallas kernels: 74.4 us -> 85.7 us  [body(): pl.pallas_call(block_kernel, out_shape=jax.ShapeDtypeStruct((2, 2, COLS,...]
    unnamed x24 -> x1, local copies, waits for them, and re-layouts: 10.3 us -> 1.84 us
    reshape x5 -> x0, local copies, waits for them, and re-layouts: 7.46 us -> none  [the longest x1 2.29 us: temporal_mix(): query_heads = queries.reshape(shape[0], -1, HEADS, HEAD_DIM)]
    slice x6 -> x0, local copies, waits for them, and re-layouts: 5.86 us -> none  [the longest x1 3.05 us: body(): halves[:, :, HALF:]]
    ppermute x2 -> x0, starting transfers between devices: 4.97 us -> none  [the longest x1 3.69 us: extended(): lax.ppermute(tail, axis, [(i, (i + 1) % count) for i in range(ends)])]
    transpose x2 -> x0, local copies, waits for them, and re-layouts: 3.82 us -> none  [half_columns(): return jnp.transpose(split, (2, 0, 1, 3)).reshape(2, 640, count * HALF)]
  transfers between devices with their start and end apart: 2 -> 0, of which waited for: 0 -> 0; matrix products, arithmetic and copies ran while one was open for 9% -> 0% of each run, Pallas kernels for 0% -> 0%
where the time goes in v2:
time: 89.3 us; the launch traced here: 87.5 us
  Pallas kernels  85.7 us (96%)
  local copies, waits for them, and re-layouts  1.84 us (2%)
    pallas_call x1, Pallas kernels, body(): pl.pallas_call(block_kernel, out_shape=jax.ShapeDtypeStruct((2, 2, COLS,...  85.7 us
    unnamed x1, local copies, waits for them, and re-layouts  1.84 us

profile of v2, /device:TPU:0, one launch (start us, length us, event | category | flops | bytes accessed | tf_op | source)
XLA Modules:
  0.0 87.5 jit_solution(8057747417669838553)
XLA Ops:
  0.0 85.7 %block.1 = f32[2,2,48,640]{3,2,1,0:T(8,128)} custom-call(bf16[2,2,48,640]{3,2,1,0:T(8,128)(2,1)} %latents_hbm.1, bf16[2,2,48,640]{3,2,1,0:T(8,128)(2,1)} %previous_hbm.1, bf16[2,2,48,640]{3,2,1,0:T(8,128)(2,1)} %stale_hbm.1, f32[3,640]{1,0:T(4,128)} %gains_ref.1, f32[2,10]{1,0:T(2,128)} %scale_ref.1, bf16[9,640,640]{2,1,0:T(8,128)(2,1)} %conv_hbm.1, ...), custom_call_target="tpu_custom_call" | custom-call | tf_op jit(solution)/shard_map/block/pallas_call | solution.py:538
  85.7 1.8 %copy.14 = f32[2,2,48,640]{3,2,1,0:T(8,128)} copy(f32[2,2,48,640]{3,2,1,0:T(8,128)} %block.1) | data formatting | bytes 983040

commit v3 on v2

v3 whole, which is shorter than its diff:
```python
import functools
import math

import jax
import jax.numpy as jnp
from jax import lax
from jax.experimental import pallas as pl
from jax.experimental.pallas import tpu as pltpu
from jax.sharding import PartitionSpec as P

HEAD_DIM = 64
NEG = -1e30
EPS = 1e-05
F32 = jnp.float32
BF16 = jnp.bfloat16
MESH = pl.DeviceIdType.MESH
NT = (((1,), (1,)), ((), ()))
WIDTH = 640
COLS = 48
PATCH = 96
QUERIES = 384
HALF = 384
HIDDEN = 2560
FF_STEP = 512
LOG2E = math.log2(math.e)

SLOTS = {
    (1, 0): (0, 0), (3, 0): (0, 1), (0, 1): (0, 2), (0, 3): (0, 3),
    (1, 1): (1, 0), (1, 3): (1, 1), (3, 1): (1, 2), (3, 3): (1, 3),
    (2, 1): (2, 0), (2, 3): (2, 1), (1, 2): (2, 2), (3, 2): (2, 3),
    (0, 0): (3, 0), (2, 0): (3, 1), (0, 2): (3, 2), (2, 2): (3, 3),
}


def dot(left, right):
    return jnp.dot(left, right, preferred_element_type=F32)


def layer_norm(values, gain):
    centre = values - jnp.mean(values, axis=-1, keepdims=True)
    spread = jnp.mean(centre * centre, axis=-1, keepdims=True)
    return (centre * lax.rsqrt(spread + EPS) * gain).astype(BF16)


def block_kernel(
    latents_hbm, previous_hbm, stale_hbm, gains_ref, scale_ref, conv_hbm, attn_hbm, attn_out_hbm,
    time_hbm, time_out_hbm, ff_in_hbm, ff_out_hbm,
    out_ref,
    lat, halo, field, conv_w, wall, attn_out_w, time_w, time_out_w, ff_in_w, ff_out_w,
    first, first_all, norm_in, kv_now, xall, q_heads, kv, scores, top, acc, peak, total,
    result, mixes, time_qkv, time_mix, third, hidden, back, back_in,
    load, recv, sent, n_recv, n_sent, r_recv, r_sent, h_recv, h_sent, l_recv, l_sent,
    f_recv, f_sent, b_recv, b_sent, local,
):
    row = lax.axis_index("rows")
    part = lax.axis_index("frames")
    core = row % 2
    z = (row // 2) % 4
    y = (row // 8) % 2
    x = row // 16

    def device(x, y, z, core, part=part):
        return (((x * 2 + y) * 4 + z) * 2 + core, part)

    def ring(along_first, step):
        dx = step * (1 - core) if along_first else step * core
        dz = step * core if along_first else step * (1 - core)
        return device((x + dx + 4) % 4, y, (z + dz + 4) % 4, core)

    a_up, a_down = ring(True, 1), ring(True, -1)
    b_up, b_down = ring(False, 1), ring(False, -1)

    def column(dc, dy, part):
        return device(x, (y + dy) % 2, z, (core + dc) % 2, part)

    mate, across = column(1, 0, part), column(0, 1, part)
    quad = [(0, 1, across), (1, 0, mate), (1, 1, column(1, 1, part))]
    partner = (row, 1 - part)
    patches = (row, row + 8 - 16 * y)

    loads = []

    def fetch(src, dst):
        copy = pltpu.make_async_copy(src, dst, load.at[len(loads)])
        loads.append(copy)
        copy.start()
        return copy

    lat_copy = fetch(latents_hbm.at[y], lat.at[0])
    conv_copies = [
        fetch(conv_hbm.at[pl.ds(3 * tap, 3)], conv_w.at[pl.ds(3 * tap, 3)]) for tap in (1, 0, 2)
    ]

    barrier = pltpu.get_barrier_semaphore()

    def greet(other):
        pl.semaphore_signal(barrier, inc=1, device_id=other, device_id_type=MESH)

    for other in (a_up, a_down, b_up, b_down) + tuple(item[2] for item in quad):
        greet(other)
    for dc in range(2):
        for dy in range(2):
            greet(column(dc, dy, 1 - part))

    for patch in patches:
        @pl.when(patch > 0)
        def _():
            greet((patch - 1, part))

        @pl.when(patch < 63)
        def _():
            greet((patch + 1, part))

    wall_copies = []
    for kind in range(3):
        wall_copies.append(fetch(
            attn_hbm.at[:, pl.ds(pl.multiple_of(WIDTH * kind + 384 * core, 128), 256)],
            wall.at[:, pl.ds(HALF * kind, 256)],
        ))
        wall_copies.append(fetch(
            attn_hbm.at[:, pl.ds(WIDTH * kind + 256, 128)],
            wall.at[:, pl.ds(HALF * kind + 256, 128)],
        ))
    late_copies = [
        fetch(attn_out_hbm, attn_out_w), fetch(time_hbm, time_w), fetch(time_out_hbm, time_out_w),
        fetch(ff_in_hbm, ff_in_w), fetch(ff_out_hbm, ff_out_w),
    ]

    @pl.when((row > 0) & (row < 63))
    def _():
        pl.semaphore_wait(barrier, 15)

    @pl.when((row == 0) | (row == 63))
    def _():
        pl.semaphore_wait(barrier, 13)

    started = []

    def remote(src, dst, send_sem, recv_sem, to):
        return pltpu.make_async_remote_copy(
            src_ref=src, dst_ref=dst, send_sem=send_sem, recv_sem=recv_sem,
            device_id=to, device_id_type=MESH,
        )

    lat_remote = remote(latents_hbm.at[1 - y], lat.at[1], l_sent.at[0], l_recv.at[0], across)
    lat_remote.start()
    edges = []
    for side in range(2):
        patch = row - 1 + 2 * side
        for frame in range(2):
            to = device(patch // 16, frame, (patch // 2) % 4, patch % 2)
            dy = ((patch // 8) % 2 + frame) % 2
            edges.append(remote(
                previous_hbm.at[frame, side], halo.at[dy, 1 - side],
                h_sent.at[side, frame], h_recv.at[dy, 1 - side], to,
            ))

    @pl.when(row > 0)
    def _():
        edges[0].start()
        edges[1].start()

    @pl.when(row < 63)
    def _():
        edges[2].start()
        edges[3].start()

    def send(src, at, to, dc=0, dy=None, places=1):
        group, place = SLOTS[at]
        if dy is not None:
            dst = xall.at[group, dc, place, dy]
        else:
            dst = xall.at[group, dc, pl.ds(place, places)]
        copy = remote(
            src, dst, sent.at[len(started)], recv.at[group, dc, place, dy or 0], to
        )
        started.append(copy)
        return copy

    def arrival(at, dc=0, dy=None, places=1):
        group, place = SLOTS[at]
        if dy is not None:
            dst = xall.at[group, dc, place, dy]
        else:
            dst = xall.at[group, dc, pl.ds(place, places)]
        sem = recv.at[group, dc, place, dy or 0]
        return lambda: remote(dst, dst, sem, sem, mate).wait_recv()

    def held(at, dy=None, places=1):
        group, place = SLOTS[at]
        if dy is not None:
            return xall.at[group, 0, place, dy]
        return xall.at[group, 0, pl.ds(place, places)]

    def arrive(at, dc=0, dy=None, places=1):
        arrival(at, dc, dy, places)()

    def own_ways(src, dy):
        return [
            send(src, (3, 0), a_up, dy=dy), send(src, (1, 0), a_down, dy=dy),
            send(src, (0, 3), b_up, dy=dy), send(src, (0, 1), b_down, dy=dy),
            send(src, (0, 0), mate, dc=1, dy=dy),
        ]

    def start(copies):
        for copy in copies:
            copy.start()

    own = stale_hbm.at[y]
    start([send(stale_hbm.at[1 - y], (0, 0), across, dy=1)])
    start(own_ways(own, 0))
    keep_own = pltpu.make_async_copy(own, held((0, 0), 0), local.at[0])
    keep_own.start()

    near_a = [
        [send(held((3, 0), 0), (2, 0), a_up, dy=0)], [send(held((1, 0), 1), (2, 0), a_down, dy=1)]
    ]
    near_b = [
        [send(held((0, 3), 0), (0, 2), b_up, dy=0)], [send(held((0, 1), 1), (0, 2), b_down, dy=1)]
    ]
    lines_b = {
        (da, dy): [
            send(held((da, 0), dy), (da, 3), b_up, dy=dy),
            send(held((da, 0), dy), (da, 1), b_down, dy=dy),
        ]
        for da in (1, 3, 2) for dy in range(2)
    }
    ahead = {
        da: [
            send(held((da, 3), 0), (da, 2), b_up, dy=0),
            send(held((da, 1), 1), (da, 2), b_down, dy=1),
        ]
        for da in (1, 3, 2)
    }
    to_mate = {
        at: [send(held(at, places=count), at, mate, dc=1, places=count)]
        for at, count in (
            ((1, 0), 2), ((0, 1), 2), ((1, 1), 2), ((3, 1), 2), ((2, 1), 2), ((1, 2), 2),
            ((2, 0), 1), ((0, 2), 1), ((2, 2), 1),
        )
    }
    dy_ways = own_ways(held((0, 0), 1), 1)

    def own_second():
        arrive((0, 0), dy=1)
        start(dy_ways)

    def near(dy):
        for da in (3, 1):
            arrive((da, 0), dy=dy)
        start(near_a[dy])
        for da in (1, 3):
            start(lines_b[da, dy])
        for db in (3, 1):
            arrive((0, db), dy=dy)
        start(near_b[dy])
        if dy == 1:
            start(to_mate[1, 0])
            start(to_mate[0, 1])

    def far_first():
        for dy in range(2):
            arrive((2, 0), dy=dy)
            start(lines_b[2, dy])
        start(to_mate[2, 0])

    def far_second():
        for dy in range(2):
            arrive((0, 2), dy=dy)
        start(to_mate[0, 2])

    def line(da):
        arrive((da, 3), dy=0)
        arrive((da, 1), dy=1)
        start(ahead[da])
        arrive((da, 3), dy=1)
        arrive((da, 1), dy=0)
        start(to_mate[da, 1])

    def lines_far():
        for da in (1, 3):
            for dy in range(2):
                arrive((da, 2), dy=dy)
        start(to_mate[1, 2])

    def last_corner():
        for dy in range(2):
            arrive((2, 2), dy=dy)
        start(to_mate[2, 2])

    column_at = lax.broadcasted_iota(jnp.int32, (COLS, WIDTH), 0)

    def fill(dy, at, values):
        cells = values.astype(F32)
        cells = cells * (1.0 / (1.0 + jnp.exp(-cells)))
        left = jnp.where(column_at == 0, 0.0, pltpu.roll(cells, 1, 0))
        right = jnp.where(column_at == COLS - 1, 0.0, pltpu.roll(cells, COLS - 1, 0))
        field[dy, at, :, :WIDTH] = left.astype(BF16)
        field[dy, at, :, WIDTH : 2 * WIDTH] = cells.astype(BF16)
        field[dy, at, :, 2 * WIDTH :] = right.astype(BF16)

    def taps(at):
        return dot(
            field[:, at : at + 2].reshape(2 * PATCH, 3 * WIDTH),
            conv_w[3 * at : 3 * at + 3].reshape(3 * WIDTH, WIDTH),
        )

    lat_copy.wait()
    fill(0, 1, lat[0, 0])
    fill(0, 2, lat[0, 1])
    for dy in range(2):
        for side in range(2):
            there = patches[dy] > 0 if side == 0 else patches[dy] < 63
            gone = patches[dy] == 0 if side == 0 else patches[dy] == 63
            edge = halo.at[dy, side]
            sem = h_recv.at[dy, side]

            @pl.when(there)
            def _():
                remote(edge, edge, sem, sem, mate).wait_recv()

            @pl.when(gone)
            def _():
                halo[dy, side] = jnp.zeros_like(halo[dy, side])

            fill(dy, 3 * side, halo[dy, side])
    lat_remote.wait_recv()
    fill(1, 1, lat[1, 0])
    fill(1, 2, lat[1, 1])
    near(0)
    own_second()
    conv_copies[0].wait()
    conv_sum = taps(1)
    conv_copies[1].wait()
    conv_sum = conv_sum + taps(0)
    conv_copies[2].wait()
    conv_sum = conv_sum + taps(2)
    start_sum = lat[...].reshape(2 * PATCH, WIDTH).astype(F32) + conv_sum
    norm_in[0] = layer_norm(start_sum, gains_ref[0:1, :]).reshape(2, PATCH, WIDTH)
    norm_copy = remote(norm_in.at[0], norm_in.at[1], n_sent.at[0], n_recv.at[0], mate)
    norm_copy.start()
    first[...] = start_sum.reshape(2, 2, COLS, WIDTH)
    frame_here = 2 * part + y
    f_copies = []
    for dy, flip in ((0, 1), (1, 0), (1, 1)):
        to_part = part + flip - 2 * part * flip
        at = 2 * dy + flip
        f_copies.append(remote(
            first.at[dy, to_part], first_all.at[frame_here], f_sent.at[at], f_recv.at[at],
            column(0, dy, to_part),
        ))
    start(f_copies)
    first_all[frame_here] = first[0, part]
    for copy in wall_copies:
        copy.wait()
    lane = lax.broadcasted_iota(jnp.int32, (QUERIES, 128), 1)
    half_lane = lax.broadcasted_iota(jnp.int32, (1, 128), 1) // HEAD_DIM

    def lane_scale(kind, pair):
        low, high = scale_ref[kind, 2 * pair], scale_ref[kind, 2 * pair + 1]
        return jnp.where(half_lane == 0, low, high) * (LOG2E / math.sqrt(HEAD_DIM))

    def project(rows, at):
        count = rows.shape[0] * rows.shape[1] * rows.shape[2] * rows.shape[3]
        kv[at : at + count] = dot(rows.reshape(count, WIDTH), wall[:, HALF:]).astype(BF16)

    keep_own.wait()
    arrive((0, 0), dc=1, dy=0)
    arrive((0, 0), dc=1, dy=1)
    for dc in range(2):
        project(xall[3, dc, 0:1], dc * 2 * PATCH)

    norm_copy.wait_recv()
    triple = dot(norm_in[...].reshape(QUERIES, WIDTH), wall[...])
    kv_now[...] = triple[:, HALF:].astype(BF16)
    for place, pair in enumerate((3 * core, 3 * core + 1, 2)):
        both = triple[:, 128 * place : 128 * place + 128] * lane_scale(0, pair)
        both = both.astype(BF16)
        zero = jnp.zeros_like(both)
        if place < 2:
            q_heads[2 * place] = jnp.where(lane < HEAD_DIM, both, zero)
            q_heads[2 * place + 1] = jnp.where(lane < HEAD_DIM, zero, both)
        else:
            q_heads[4] = jnp.where(lane // HEAD_DIM == core, both, zero)
    acc[...] = jnp.zeros_like(acc)
    total[...] = jnp.zeros_like(total)
    peak[...] = jnp.full_like(peak, NEG)

    def attend(keys, masked, hooks):
        def keys_of(head):
            at = 128 * (head // 2)
            return kv[:keys, at : at + 128]

        def score(head):
            s = lax.dot_general(q_heads[head], keys_of(head), NT, preferred_element_type=F32)
            if masked:
                q_patch = lax.broadcasted_iota(jnp.int32, (QUERIES, keys), 0) // PATCH
                k_patch = lax.broadcasted_iota(jnp.int32, (QUERIES, keys), 1) // PATCH
                drop = ((k_patch < 4) & (k_patch == q_patch)) | (
                    (k_patch >= 4) & (k_patch != q_patch + 4)
                )
                s = jnp.where(drop, NEG, s)
            scores[head % 2, :, :keys] = s
            top[head % 2] = jnp.broadcast_to(jnp.max(s, axis=1, keepdims=True), (QUERIES, 128))

        score(0)
        for head in range(5):
            if head in hooks:
                hooks[head]()
            if head < 4:
                score(head + 1)
            pair = head // 2
            old = peak[head]
            new = jnp.maximum(old, top[head % 2])
            factor = jnp.exp2(old - new)
            peak[head] = new
            w = jnp.exp2(scores[head % 2, :, :keys] - new[:, :1])
            total[head] = total[head] * factor + jnp.sum(w, axis=1, keepdims=True)
            at = HALF + 128 * pair
            part_sum = dot(w.astype(BF16), kv[:keys, at : at + 128])
            if head == 4:
                acc[pair] = acc[pair] * factor + part_sum
            else:
                here = (lane < HEAD_DIM) if head % 2 == 0 else (lane >= HEAD_DIM)
                acc[pair] = acc[pair] * jnp.where(here, factor, 1.0) + jnp.where(
                    here, part_sum, 0.0
                )

    kv[4 * PATCH : 8 * PATCH] = kv_now[...]
    attend(8 * PATCH, True, {1: functools.partial(near, 1), 4: far_first})

    def group(g):
        def when(table):
            def hook():
                for at, actions in table.items():
                    if g == at:
                        for action in actions:
                            action()
            return hook

        when({
            0: [arrival((1, 0), 1, None, 2), arrival((0, 1), 1, None, 2)],
            1: [arrival((1, 1), 1, None, 2), arrival((3, 1), 1, None, 2)],
            2: [arrival((2, 1), 1, None, 2), arrival((1, 2), 1, None, 2)],
        })()
        for dc in range(2):
            project(xall[g, dc], dc * 8 * PATCH)
        attend(16 * PATCH, False, {
            0: when({0: [far_second]}),
            2: when({0: [functools.partial(line, 1)], 1: [lines_far]}),
            3: when({0: [functools.partial(line, 3)], 1: [last_corner]}),
            4: when({0: [functools.partial(line, 2)]}),
        })

    for g in range(3):
        group(g)
    arrive((2, 0), 1)
    arrive((0, 2), 1)
    arrive((2, 2), 1)
    for dc in range(2):
        project(xall[3, dc, 1:4], dc * 6 * PATCH)

    r_copies = []

    def deliver(pairs):
        for pair in pairs:
            below = total[2 * pair]
            if pair < 2:
                below = jnp.where(lane < HEAD_DIM, below, total[2 * pair + 1])
            mixed = acc[pair] / below
            if pair == 2:
                mixed = jnp.where(lane // HEAD_DIM == core, mixed, 0.0)
            lanes = slice(128 * pair, 128 * pair + 128)
            result[:, :, :, lanes] = mixed.astype(BF16).reshape(4, 2, COLS, 128)
        lanes = pl.ds(128 * pairs[0], 128 * len(pairs))
        frame = 2 * part + y
        for flip, dc, dy in (
            (1, 1, 1), (1, 0, 1), (1, 1, 0), (1, 0, 0), (0, 1, 1), (0, 0, 1), (0, 1, 0)
        ):
            to_part = part + flip - 2 * part * flip
            at = len(r_copies)
            r_copies.append(remote(
                result.at[2 * dc + dy, to_part, :, lanes], mixes.at[frame, core, :, lanes],
                r_sent.at[at], r_recv.at[at], column(dc, dy, to_part),
            ))
            r_copies[-1].start()
        mixes[frame, core, :, lanes] = result[0, part, :, lanes]

    attend(12 * PATCH, False, {4: functools.partial(deliver, (0, 1))})
    deliver((2,))
    for copy in f_copies:
        copy.wait_recv()
    for copy in late_copies:
        copy.wait()
    for copy in r_copies:
        copy.wait_recv()

    rows = 4 * COLS
    middle = mixes[:, 0, :, 256:] + mixes[:, 1, :, 256:]
    mix = jnp.concatenate(
        [mixes[:, 0, :, :256], middle, mixes[:, 1, :, :256]], axis=-1
    ).reshape(rows, WIDTH)
    second = first_all[...].reshape(rows, WIDTH) + dot(mix, attn_out_w[...])
    third[...] = second
    time_qkv[...] = dot(layer_norm(second, gains_ref[1:2, :]), time_w[...]).astype(BF16)

    ones_row = lax.broadcasted_iota(jnp.int32, (256, 128), 0) % 128 // HEAD_DIM
    ones_col = lax.broadcasted_iota(jnp.int32, (256, 128), 1) // HEAD_DIM
    ones = jnp.where(ones_row == ones_col, 1.0, 0.0).astype(BF16)
    for pair in range(5):
        def lanes_of(kind):
            at = WIDTH * kind + 128 * pair
            return time_qkv[:, at : at + 128].reshape(4, COLS, 128).astype(F32)

        tq, tk, tv = lanes_of(0), lanes_of(1), lanes_of(2)
        products = (tq[:, None] * tk[None]).reshape(16 * COLS, 128)
        high = products.astype(BF16)
        low = (products - high.astype(F32)).astype(BF16)
        s = dot(jnp.concatenate([high, low], axis=1), ones) * lane_scale(1, pair)
        s = s.reshape(4, 4, COLS, 128)
        w = jnp.exp2(s - jnp.max(s, axis=1, keepdims=True))
        mixed = jnp.sum(w.astype(BF16).astype(F32) * tv[None], axis=1) / jnp.sum(w, axis=1)
        time_mix[:, 128 * pair : 128 * pair + 128] = mixed.astype(BF16).reshape(rows, 128)
    third[...] = third[...] + dot(time_mix[...], time_out_w[...])
    normed_three = layer_norm(third[...], gains_ref[2:3, :])
    for step in range(HIDDEN // FF_STEP):
        at = FF_STEP * step
        value = dot(normed_three, ff_in_w[:, at : at + FF_STEP])
        gate = dot(normed_three, ff_in_w[:, HIDDEN + at : HIDDEN + at + FF_STEP])
        gelu = 0.5 * gate * (1.0 + lax.erf(gate * math.sqrt(0.5)))
        hidden[:, at : at + FF_STEP] = (value * gelu).astype(BF16)
    half_rows = 2 * COLS
    mine = pl.ds(pl.multiple_of(part * half_rows, half_rows), half_rows)
    theirs = pl.ds(pl.multiple_of((1 - part) * half_rows, half_rows), half_rows)
    b_copies = []
    for at, count in ((0, 384), (384, 256)):
        lanes = slice(at, at + count)
        third[:, lanes] = third[:, lanes] + dot(hidden[...], ff_out_w[:, lanes])
        back[:, lanes] = third[theirs, lanes].astype(BF16)
        ref = pl.ds(at, count)
        b_copies.append(remote(
            back.at[:, ref], back_in.at[:, ref], b_sent.at[len(b_copies)],
            b_recv.at[len(b_copies)], partner,
        ))
        b_copies[-1].start()
    out_ref[:, part] = third[mine].reshape(2, COLS, WIDTH)
    for copy in b_copies:
        copy.wait_recv()
    out_ref[:, 1 - part] = back_in[...].astype(F32).reshape(2, COLS, WIDTH)
    for copy in started + r_copies + f_copies + b_copies + [norm_copy, lat_remote]:
        copy.wait_send()

    @pl.when(row > 0)
    def _():
        edges[0].wait_send()
        edges[1].wait_send()

    @pl.when(row < 63)
    def _():
        edges[2].wait_send()
        edges[3].wait_send()


def body(*arrays):
    vmem = pl.BlockSpec(memory_space=pltpu.VMEM)
    hbm = pl.BlockSpec(memory_space=pl.ANY)
    dma = pltpu.SemaphoreType.DMA
    rows = 4 * COLS
    return pl.pallas_call(
        block_kernel,
        out_shape=jax.ShapeDtypeStruct((2, 2, COLS, WIDTH), F32),
        in_specs=[hbm] * 3 + [vmem, pl.BlockSpec(memory_space=pltpu.SMEM)] + [hbm] * 7,
        out_specs=vmem,
        scratch_shapes=[
            pltpu.VMEM((2, 2, COLS, WIDTH), BF16),
            pltpu.VMEM((2, 2, COLS, WIDTH), BF16),
            pltpu.VMEM((2, 4, COLS, 3 * WIDTH), BF16),
            pltpu.VMEM((9, WIDTH, WIDTH), BF16),
            pltpu.VMEM((WIDTH, 3 * HALF), BF16),
            pltpu.VMEM((WIDTH, WIDTH), BF16),
            pltpu.VMEM((WIDTH, 3 * WIDTH), BF16),
            pltpu.VMEM((WIDTH, WIDTH), BF16),
            pltpu.VMEM((WIDTH, 2 * HIDDEN), BF16),
            pltpu.VMEM((HIDDEN, WIDTH), BF16),
            pltpu.VMEM((2, 2, COLS, WIDTH), F32),
            pltpu.VMEM((4, COLS, WIDTH), F32),
            pltpu.VMEM((2, 2, PATCH, WIDTH), BF16),
            pltpu.VMEM((QUERIES, 2 * HALF), BF16),
            pltpu.VMEM((4, 2, 4, 2, 2, COLS, WIDTH), BF16),
            pltpu.VMEM((5, QUERIES, 128), BF16),
            pltpu.VMEM((16 * PATCH, 2 * HALF), BF16),
            pltpu.VMEM((2, QUERIES, 16 * PATCH), F32),
            pltpu.VMEM((2, QUERIES, 128), F32),
            pltpu.VMEM((3, QUERIES, 128), F32),
            pltpu.VMEM((5, QUERIES, 128), F32),
            pltpu.VMEM((5, QUERIES, 128), F32),
            pltpu.VMEM((4, 2, COLS, HALF), BF16),
            pltpu.VMEM((4, 2, COLS, HALF), BF16),
            pltpu.VMEM((rows, 3 * WIDTH), BF16),
            pltpu.VMEM((rows, WIDTH), BF16),
            pltpu.VMEM((rows, WIDTH), F32),
            pltpu.VMEM((rows, HIDDEN), BF16),
            pltpu.VMEM((PATCH, WIDTH), BF16),
            pltpu.VMEM((PATCH, WIDTH), BF16),
            dma((15,)),
            dma((4, 2, 4, 2)),
            dma((48,)),
            dma((1,)),
            dma((1,)),
            dma((14,)),
            dma((14,)),
            dma((2, 2)),
            dma((2, 2)),
            dma((1,)),
            dma((1,)),
            dma((4,)),
            dma((4,)),
            dma((2,)),
            dma((2,)),
            dma((1,)),
        ],
        compiler_params=pltpu.CompilerParams(
            collective_id=0, has_side_effects=True, vmem_limit_bytes=62 << 20
        ),
        name="block",
    )(*arrays)


def solution(mesh):
    split = P("frames", "rows", None, None)
    return jax.shard_map(
        body,
        mesh=mesh,
        in_specs=(split,) * 3 + (P(),) * 9,
        out_specs=split,
        check_vma=False,
    )
```

time: 89.3 us -> 74 us (0.83)
  Pallas kernels: 85.7 us -> 71 us
    pallas_call x1, Pallas kernels: 85.7 us -> 71 us  [body(): pl.pallas_call(block_kernel, out_shape=jax.ShapeDtypeStruct((2, 2, COLS,...]
where the time goes in v3:
time: 74 us; the launch traced here: 72.8 us
  Pallas kernels  71 us (96%)
  local copies, waits for them, and re-layouts  1.84 us (2%)
    pallas_call x1, Pallas kernels, body(): pl.pallas_call(block_kernel, out_shape=jax.ShapeDtypeStruct((2, 2, COLS,...  71 us
    unnamed x1, local copies, waits for them, and re-layouts  1.84 us

profile of v3, /device:TPU:0, one launch (start us, length us, event | category | flops | bytes accessed | tf_op | source)
XLA Modules:
  0.0 72.8 jit_solution(233806348829136572)
XLA Ops:
  0.0 71.0 %block.1 = f32[2,2,48,640]{3,2,1,0:T(8,128)} custom-call(bf16[2,2,48,640]{3,2,1,0:T(8,128)(2,1)} %latents_hbm.1, bf16[2,2,48,640]{3,2,1,0:T(8,128)(2,1)} %previous_hbm.1, bf16[2,2,48,640]{3,2,1,0:T(8,128)(2,1)} %stale_hbm.1, f32[3,640]{1,0:T(4,128)} %gains_ref.1, f32[2,10]{1,0:T(2,128)} %scale_ref.1, bf16[9,640,640]{2,1,0:T(8,128)(2,1)} %conv_hbm.1, ...), custom_call_target="tpu_custom_call" | custom-call | tf_op jit(solution)/shard_map/block/pallas_call | solution.py:569
  71.0 1.8 %copy.14 = f32[2,2,48,640]{3,2,1,0:T(8,128)} copy(f32[2,2,48,640]{3,2,1,0:T(8,128)} %block.1) | data formatting | bytes 983040

commit v4 on v3

--- a/solution.py
+++ b/solution.py
@@ -438,13 +438,13 @@
                             action()
             return hook
 
+        project(xall[g, 0], 0)
         when({
             0: [arrival((1, 0), 1, None, 2), arrival((0, 1), 1, None, 2)],
             1: [arrival((1, 1), 1, None, 2), arrival((3, 1), 1, None, 2)],
             2: [arrival((2, 1), 1, None, 2), arrival((1, 2), 1, None, 2)],
         })()
-        for dc in range(2):
-            project(xall[g, dc], dc * 8 * PATCH)
+        project(xall[g, 1], 8 * PATCH)
         attend(16 * PATCH, False, {
             0: when({0: [far_second]}),
             2: when({0: [functools.partial(line, 1)], 1: [lines_far]}),
@@ -454,11 +454,11 @@
 
     for g in range(3):
         group(g)
+    project(xall[3, 0, 1:4], 0)
     arrive((2, 0), 1)
     arrive((0, 2), 1)
     arrive((2, 2), 1)
-    for dc in range(2):
-        project(xall[3, dc, 1:4], dc * 6 * PATCH)
+    project(xall[3, 1, 1:4], 6 * PATCH)
 
     r_copies = []
 
@@ -486,7 +486,9 @@
             r_copies[-1].start()
         mixes[frame, core, :, lanes] = result[0, part, :, lanes]
 
-    attend(12 * PATCH, False, {4: functools.partial(deliver, (0, 1))})
+    attend(12 * PATCH, False, {
+        2: functools.partial(deliver, (0,)), 4: functools.partial(deliver, (1,)),
+    })
     deliver((2,))
     for copy in f_copies:
         copy.wait_recv()
@@ -607,8 +609,8 @@
             dma((48,)),
             dma((1,)),
             dma((1,)),
-            dma((14,)),
-            dma((14,)),
+            dma((21,)),
+            dma((21,)),
             dma((2, 2)),
             dma((2, 2)),
             dma((1,)),

time: 74 us -> 74.2 us (level)
  the two profiles are of different devices: /device:TPU:0 before, /device:TPU:6 now
where the time goes in v4:
time: 74.2 us; the launch traced here: 74 us
  Pallas kernels  72.1 us (97%)
  local copies, waits for them, and re-layouts  1.84 us (2%)
    pallas_call x1, Pallas kernels, body(): pl.pallas_call(block_kernel, out_shape=jax.ShapeDtypeStruct((2, 2, COLS,...  72.1 us
    unnamed x1, local copies, waits for them, and re-layouts  1.84 us

profile of v4, /device:TPU:6, one launch (start us, length us, event | category | flops | bytes accessed | tf_op | source)
XLA Modules:
  0.0 74.0 jit_solution(3984270923085772276)
XLA Ops:
  0.0 72.1 %block.1 = f32[2,2,48,640]{3,2,1,0:T(8,128)} custom-call(bf16[2,2,48,640]{3,2,1,0:T(8,128)(2,1)} %latents_hbm.1, bf16[2,2,48,640]{3,2,1,0:T(8,128)(2,1)} %previous_hbm.1, bf16[2,2,48,640]{3,2,1,0:T(8,128)(2,1)} %stale_hbm.1, f32[3,640]{1,0:T(4,128)} %gains_ref.1, f32[2,10]{1,0:T(2,128)} %scale_ref.1, bf16[9,640,640]{2,1,0:T(8,128)(2,1)} %conv_hbm.1, ...), custom_call_target="tpu_custom_call" | custom-call | tf_op jit(solution)/shard_map/block/pallas_call | solution.py:571
  72.1 1.8 %copy.14 = f32[2,2,48,640]{3,2,1,0:T(8,128)} copy(f32[2,2,48,640]{3,2,1,0:T(8,128)} %block.1) | data formatting | bytes 983040
